TPU v7x, 512 devices: a whole 4x8x8 slice. The times are simulated.
512 devices in a mesh: ctx: 128 (over y, z, core), kvh: 4 (over x).
Axes of the slice: x: 4, y: 8, z: 8, core: 2. Of those that a mesh axis runs over, the one named last changes fastest.
Arguments:
- hidden: bfloat16 [3, 4, 4096], P(None, None, 'ctx'), may hold values from -6 to 6
- w_query: bfloat16 [4096, 8192], P('ctx', 'kvh'), may hold values from -0.09375 to 0.09375
- q_gain: float32 [128], replicated, may hold values from 0.25 to 1.75
- basis: float32 [4, 128, 128], P('kvh'), may hold values from -0.5 to 0.5
- keys: bfloat16 [4, 4, 196608, 128], P(None, 'kvh', 'ctx'), may hold values from -2500 to 2500
- values: bfloat16 [4, 4, 196608, 128], P(None, 'kvh', 'ctx'), may hold values from -6 to 6
- new_keys: bfloat16 [3, 4, 4, 128], P(None, None, 'kvh'), may hold values from -25 to 25
- new_values: bfloat16 [3, 4, 4, 128], P(None, None, 'kvh'), may hold values from -6 to 6
- block_lists: int32 [3, 4, 4, 256], P(None, None, 'kvh'), may hold values from 0 to 1535, as said below
- w_out: bfloat16 [8192, 4096], P('kvh', 'ctx'), may hold values from -0.5 to 0.5
Outputs:
- block_logmass: float32 [3, 4, 64, 1536], P(None, None, 'kvh', 'ctx')
- layer_out: bfloat16 [3, 4, 4096], P(None, None, 'ctx')
Inputs may be any that keep to these rules, and one draw needn't show every extreme that they name: `block_lists`: each list holds 256 distinct block numbers in ascending order. Counted per index of ctx (blocks i * 12 to i * 12 + 11), a list has at most 8 of them there, and in every list some index holds exactly 8.
All inputs are finite; a program needn't handle non-finite values.
Results may differ from a plain program's by a relative error of at most 0.017.
Values may be sent and summed in bfloat16 or wider, within the bound.
A program may use at most 128 MiB of HBM per device.

v0:
```python
import jax
import jax.numpy as jnp
from jax import lax
from jax.sharding import PartitionSpec as P

RANK = 32
BLK = 128


def body(hidden, w_query, q_gain, basis, keys, values, new_keys, new_values, block_lists, w_out):
    highest = lax.Precision.HIGHEST
    n_reqs = hidden.shape[1]
    head_dim = basis.shape[1]
    groups = w_query.shape[1] // head_dim
    local_tok = keys.shape[2]
    n_local = local_tok // BLK
    scale = head_dim ** (-0.5)
    first_block = lax.axis_index("ctx") * n_local
    key_local = keys[:, 0]
    val_local = values[:, 0]
    key_low = key_local[:, :, :RANK].astype(jnp.float32)
    fresh_keys = new_keys[:, :, 0].astype(jnp.float32)
    fresh_vals = new_values[:, :, 0]
    n_steps = fresh_keys.shape[0]
    mass_parts = []
    out_parts = []
    for step_no in range(n_steps):
        hid_rows = hidden[step_no : step_no + 1]
        n_rows = hid_rows.shape[0]
        query = lax.psum(
            jnp.dot(
                hid_rows.reshape(n_rows * n_reqs, -1), w_query, preferred_element_type=jnp.float32
            ),
            "ctx",
        )
        query = query.reshape(n_rows, n_reqs, groups, head_dim)
        normed = query * lax.rsqrt(jnp.mean(query * query, axis=-1, keepdims=True) + 1e-06) * q_gain
        q_rot = jnp.einsum("srgd,de->srge", normed, basis[0], precision=highest)
        low_score = (
            jnp.einsum("srgc,rtc->srgt", q_rot[..., :RANK], key_low, precision=highest) * scale
        )
        blocked = low_score.reshape(n_rows, n_reqs, groups, n_local, BLK)
        block_top = jnp.max(blocked, axis=-1)
        block_lse = block_top + jnp.log(jnp.sum(jnp.exp(blocked - block_top[..., None]), axis=-1))
        low_top = jnp.max(block_lse, axis=-1)
        low_sum = jnp.sum(jnp.exp(block_lse - low_top[..., None]), axis=-1)
        local_ids = first_block + jnp.arange(n_local, dtype=jnp.int32)
        block_mask = jnp.any(
            block_lists[step_no : step_no + 1, :, 0][..., :, None] == local_ids, axis=-2
        )
        token_mask = jnp.repeat(block_mask, BLK, axis=-1)[:, :, None, :]
        exact = (
            jnp.einsum("srgd,rtd->srgt", q_rot, key_local.astype(jnp.float32), precision=highest)
            * scale
        )
        exact = jnp.where(token_mask, exact, -1e30)
        exact_top = jnp.max(exact, axis=-1)
        probs = jnp.where(token_mask, jnp.exp(exact - exact_top[..., None]), 0.0)
        acc = jnp.einsum(
            "srgt,rtd->srgd",
            probs.astype(jnp.bfloat16),
            val_local,
            preferred_element_type=jnp.float32,
        )
        exact_sum = jnp.sum(probs, axis=-1)
        glob_low, glob_exact = lax.pmax((low_top, exact_top), "ctx")
        shrink = jnp.exp(exact_top - glob_exact)
        low_sum, exact_sum, acc = lax.psum(
            (low_sum * jnp.exp(low_top - glob_low), exact_sum * shrink, acc * shrink[..., None]),
            "ctx",
        )
        low_top = glob_low
        exact_top = glob_exact
        compute_logmass = block_lse - (low_top + jnp.log(low_sum))[..., None]
        fresh = jnp.einsum("srgd,trd->srgt", q_rot, fresh_keys, precision=highest) * scale
        seen = (
            jnp.arange(n_steps, dtype=jnp.int32)[None, :]
            <= jnp.full((1,), step_no, jnp.int32)[:, None]
        )[:, None, None, :]
        fresh = jnp.where(seen, fresh, -1e30)
        top = jnp.maximum(exact_top, jnp.max(fresh, axis=-1))
        old_scale = jnp.exp(exact_top - top)
        new_w = jnp.where(seen, jnp.exp(fresh - top[..., None]), 0.0)
        total = exact_sum * old_scale + jnp.sum(new_w, axis=-1)
        acc = acc * old_scale[..., None] + jnp.einsum(
            "srgt,trd->srgd",
            new_w.astype(jnp.bfloat16),
            fresh_vals,
            preferred_element_type=jnp.float32,
        )
        attn = (acc / total[..., None]).astype(jnp.bfloat16)
        out_terms = jnp.dot(
            attn.reshape(n_rows * n_reqs, groups * head_dim),
            w_out,
            preferred_element_type=jnp.float32,
        ).astype(jnp.bfloat16)
        compute_layer_out = lax.psum(out_terms, "kvh").astype(jnp.float32).astype(jnp.bfloat16)
        out_one = compute_layer_out.reshape(n_rows, n_reqs, -1)
        mass_parts.append(compute_logmass)
        out_parts.append(out_one)
    logmass = jnp.concatenate(mass_parts, axis=0)
    layer_out = jnp.concatenate(out_parts, axis=0)
    return (logmass, layer_out)


def solution(mesh):
    placed = (
        P(None, None, "ctx"),
        P("ctx", "kvh"),
        P(),
        P("kvh", None, None),
        P(None, "kvh", "ctx", None),
        P(None, "kvh", "ctx", None),
        P(None, None, "kvh", None),
        P(None, None, "kvh", None),
        P(None, None, "kvh", None),
        P("kvh", "ctx"),
    )
    return jax.shard_map(
        body,
        mesh=mesh,
        in_specs=placed,
        out_specs=(P(None, None, "kvh", "ctx"), P(None, None, "ctx")),
        check_vma=False,
    )
```

profile of v0, /device:TPU:1, one launch (start us, length us, event | category | flops | bytes accessed | tf_op | source)
XLA Modules:
  0.0 932.9 jit_solution(1083174581556526755)
XLA Ops:
  7.2 1.8 fusion.153
  9.0 1.7 fusion.155
  10.7 1.7 fusion.157
  16.7 1.7 copy.49
  19.1 180.2 %all-reduce.9.cloned.1.call-done = (f32[4,2048]{1,0:T(4,128)}, f32[4,2048]{1,0:T(4,128)}, f32[4,2048]{1,0:T(4,128)}) async-done(((f32[4,2048]{1,0:T(4,128)}, f32[4,2048]{1,0:T(4,128)}, f32[4,2048]{1,0:T(4,128)}), (f32[4,2048]{1,0:T(4,128)}, f32[4,2048]{1,0:T(4,128)}, f32[4,2048]{1,0:T(4,128)})) %all-reduce.9.cloned.1.call-update) | async-done | bytes 98320 | tf_op jit(solution)/shard_map/psum | solution.py:30
  202.2 1.5 fusion.113
  206.5 1.0 fusion.100
  210.3 1.0 fusion.96
  214.0 1.9 reduce_max.129
  215.8 1.9 reduce_max.126
  217.7 1.3 reduce_max.132
  219.0 1.4 exponential_reduce_fusion
  220.6 1.4 fusion.180
  222.1 1.4 fusion.179
  223.6 2.0 fusion.178
  227.9 485.9 %all-reduce.2 = (f32[1,4,16]{2,1,0:T(4,128)S(1)}, f32[1,4,16]{2,1,0:T(4,128)S(1)}, f32[1,4,16]{2,1,0:T(4,128)S(1)}, f32[1,4,16]{2,1,0:T(4,128)S(1)}, f32[1,4,16]{2,1,0:T(4,128)S(1)}, /*index=5*/f32[1,4,16]{2,1,0:T(4,128)S(1)}) all-reduce(f32[1,4,16]{2,1,0:T(4,128)} %bitcast.488, ...), channel_id=1, replica_groups=mesh['ctx'=128,'kvh'=4] {'ctx'}, use_global_device_ids=true, to_apply=%region_21.22 | all-reduce | flops 384 | bytes 3072 | tf_op jit(solution)/shard_map/pmax | solution.py:66
  713.8 1.3 bitcast_multiply_fusion.5
  715.1 2.0 fusion.51
  719.7 1.0 fusion.39
  722.7 185.7 %all-reduce.7.cloned.1.call-done = (f32[1,4,16]{2,1,0:T(4,128)}, f32[1,4,16]{2,1,0:T(4,128)}, f32[1,4,16]{2,1,0:T(4,128)}, f32[1,4,16,128]{3,2,1,0:T(8,128)}, f3...) async-done(((f32[1,4,16]{2,1,0:T(4,128)}, f32[1,4,16]{2,1,0:T(4,128)}, ...) | async-done | bytes 99856 | tf_op jit(solution)/shard_map/psum | solution.py:68
  909.2 1.0 fusion.57
  911.0 1.0 fusion.58
  912.9 1.0 fusion.59
  917.1 8.4 all-reduce.3
  (169 shorter events, 29.2 us)
Async XLA Ops:
  7.2 707.9 %copy-start = (bf16[4,1,1536,128]{3,2,1,0:T(8,128)(2,1)S(1)}, bf16[4,1,1536,128]{3,2,1,0:T(8,128)(2,1)}, u32[]{:S(2)}) copy-start(bf16[4,1,1536,128]{3,2,1,0:T(8,128)(2,1)} %param.15) | copy-start | bytes 4718596
  7.2 192.2 %all-reduce.9.cloned.1.call-start = ((), (), s32[]{:S(2)}) async-start(), calls=%async_computation.1 | async-start | bytes 196608 | tf_op jit(solution)/shard_map/psum | solution.py:30
  12.3 896.1 %all-reduce.7.cloned.1.call-start = ((), (), s32[]{:S(2)}) async-start(), calls=%async_computation | async-start | bytes 221184 | tf_op jit(solution)/shard_map/psum | solution.py:68
  16.7 186.9 %copy-start.14 = (f32[1,128,128]{2,1,0:T(8,128)S(1)}, f32[1,128,128]{2,1,0:T(8,128)}, u32[]{:S(2)}) copy-start(f32[1,128,128]{2,1,0:T(8,128)} %param.13) | copy-start | bytes 196612
  213.1 7.4 copy-start.1
  214.0 6.6 copy-start.24
  214.0 6.6 copy-start.26
  217.7 4.3 copy-start.21
  219.0 4.5 copy-start.7
  220.4 6.8 copy-start.15
  220.5 6.7 copy-start.33
  222.0 5.4 copy-start.32
  222.0 5.9 copy-start.4
  223.5 4.1 copy-start.2
  223.5 4.1 copy-start.30
  225.6 489.5 %copy-start.28 = (pred[1,4,12,128]{3,1,2,0:T(4,128)(4,1)S(1)}, pred[1,4,12,128]{3,1,2,0:T(4,128)(4,1)}, u32[]{:S(2)}) copy-start(pred[1,4,12,128]{3,1,2,0:T(4,128)(4,1)} %copy.146) | copy-start | bytes 18436
  227.8 489.2 %copy-start.31 = (f32[4,16]{1,0:T(4,128)S(1)}, f32[4,16]{1,0:T(4,128)}, u32[]{:S(2)}) copy-start(f32[4,16]{1,0:T(4,128)} %copy-done.30) | copy-start | bytes 772
  227.9 489.8 %copy-start.3 = (f32[1,4,16,1536]{3,2,1,0:T(8,128)S(1)}, f32[1,4,16,1536]{3,2,1,0:T(8,128)}, u32[]{:S(2)}) copy-start(f32[1,4,16,1536]{3,2,1,0:T(8,128)} %copy-done.2) | copy-start | bytes 1179652
  718.7 190.5 %copy-start.43 = (bf16[3,4,1,128]{3,1,2,0:T(4,128)(2,1)S(1)}, bf16[3,4,1,128]{3,1,2,0:T(4,128)(2,1)}, u32[]{:S(2)}) copy-start(bf16[3,4,1,128]{3,1,2,0:T(4,128)(2,1)} %param.17) | copy-start | bytes 9220
  718.7 191.5 %copy-start.40 = (bf16[2048,32]{0,1:T(8,128)(2,1)S(1)}, bf16[2048,32]{0,1:T(8,128)(2,1)}, u32[]{:S(2)}) copy-start(bf16[2048,32]{0,1:T(8,128)(2,1)} %param.19) | copy-start | bytes 393220
  719.7 195.0 %copy-start.13 = (f32[4,16,12]{2,1,0:T(8,128)S(1)}, f32[4,16,12]{2,1,0:T(8,128)}, u32[]{:S(2)}) copy-start(f32[4,16,12]{2,1,0:T(8,128)} %reduce_max.126) | copy-start | bytes 9220
  719.7 195.8 %copy-start.11 = (f32[4,16,12]{2,1,0:T(8,128)S(1)}, f32[4,16,12]{2,1,0:T(8,128)}, u32[]{:S(2)}) copy-start(f32[4,16,12]{2,1,0:T(8,128)} %reduce_max.129) | copy-start | bytes 9220
  719.7 196.5 %copy-start.9 = (f32[4,16,12]{2,1,0:T(8,128)S(1)}, f32[4,16,12]{2,1,0:T(8,128)}, u32[]{:S(2)}) copy-start(f32[4,16,12]{2,1,0:T(8,128)} %copy-done.7) | copy-start | bytes 9220
  719.7 196.5 %copy-start.16 = (f32[4,16,12]{2,1,0:T(8,128)S(1)}, f32[4,16,12]{2,1,0:T(8,128)}, u32[]{:S(2)}) copy-start(f32[4,16,12]{2,1,0:T(8,128)} %copy-done.15) | copy-start | bytes 9220
  (22 other events, 60.8 us)
Sparse Core Ops, SparseCore 0:
  12.5 186.8 all-reduce.8
  722.8 185.6 all-reduce.6
where the time goes:
time: 935 us; the launch traced here: 933 us
  blocking collectives  494 us (53%)
  waiting for transfers between devices  366 us (39%)
  other arithmetic  24.4 us (3%)
  matrix products  21 us (2%)
  between operations  14.6 us (2%)
  local copies, waits for them, and re-layouts  12.6 us (1%)
    pmax x1, blocking collectives, body(): glob_low, glob_exact = lax.pmax((low_top, exact_top), 'ctx')  486 us
    psum x1, waiting for transfers between devices, body(): lax.psum((low_sum * jnp.exp(low_top - glob_low), exact_sum * shrink, acc...  186 us
    psum x1, waiting for transfers between devices, body(): lax.psum(jnp.dot(hid_rows.reshape(n_rows * n_reqs, -1), w_query, preferre...  180 us
  transfers between devices with their start and end apart: 2, of which 2 were waited for; matrix products, arithmetic and copies ran while one was open for 1% of the time, Pallas kernels for 0%

commit v1 on v0

v1 whole, which is shorter than its diff:
```python
import jax
import jax.numpy as jnp
from jax import lax
from jax.experimental import pallas as pl
from jax.experimental.pallas import tpu as pltpu
from jax.sharding import PartitionSpec as P

RANK = 32
BLK = 128
STEPS = 3
REQ = 4
ROWS = STEPS * REQ
SLOT = 16
STAT = 12
LOW = 16
HEADS = 16
HALF = 8
HD = 128
NONE = -1e30
MESH = pl.DeviceIdType.MESH
F32 = jnp.float32
BF16 = jnp.bfloat16


def split3(x):
    hi = x.astype(BF16)
    rest = x - hi.astype(F32)
    mid = rest.astype(BF16)
    lo = (rest - mid.astype(F32)).astype(BF16)
    return hi, mid, lo


def slot(i):
    if isinstance(i, int):
        return pl.ds(i * SLOT, SLOT)
    return pl.ds(pl.multiple_of(i * SLOT, SLOT), SLOT)


def iota(shape, dim):
    return lax.broadcasted_iota(jnp.int32, shape, dim)


def column(row):
    diag = iota((SLOT, HD), 0) == iota((SLOT, HD), 1)
    return jnp.sum(jnp.where(diag, row, 0.0), axis=1, keepdims=True)


def kernel(
    hid_h, wq_h, gain_h, basis_h, keys_h, vals_h, nk_h, nv_h, lists_h, wo_h,
    mass_o, out_o,
    hid_v, wq_v, gain_v, basis_v, keys_v, vals_v, nk_v, nv_v, lists_v, wo_v,
    list_rows, bias, nk_rows, nv_rows, rot,
    q_part, q_core, q_half, q_rs, q_own, q_ex, q_all,
    o_part, o_core, o_half, o_rs, o_own, o_ex, o_all, lse_all,
    x_own, x_in,
    in_sem, core_s, core_r, rs_s, rs_r, ex_s, ex_r, ag_s, ag_r, x_s, x_r,
):
    ctx = lax.axis_index("ctx")
    x = lax.axis_index("kvh")
    y = ctx // 16
    z = lax.rem(ctx // 2, 8)
    c = lax.rem(ctx, 2)
    a = z + c * (y - z)
    b = y + c * (z - y)
    mine = c * HALF

    def at(aa, bb, cc):
        yy = bb + c * (aa - bb)
        zz = aa + c * (bb - aa)
        return ((yy * 8 + zz) * 2 + cc, x)

    sibling = (ctx + 1 - 2 * c, x)

    def ring_a(k):
        return lax.rem(a + k, HALF)

    def ring_b(k):
        return lax.rem(b + k, HALF)

    def dev_a(k):
        return at(ring_a(k), b, c)

    def dev_b(k):
        return at(a, ring_b(k), c)

    def dev_x(k):
        return (ctx, lax.rem(x + k, 4))

    pairs = (
        (hid_h, hid_v), (wq_h, wq_v), (gain_h, gain_v), (basis_h, basis_v), (lists_h, lists_v),
        (nk_h, nk_v), (nv_h, nv_v), (keys_h, keys_v), (vals_h, vals_v), (wo_h, wo_v),
    )
    fetch = [pltpu.make_async_copy(s, d, in_sem.at[i]) for i, (s, d) in enumerate(pairs)]
    for one in fetch:
        one.start()
    barrier = pltpu.get_barrier_semaphore()
    partners = [sibling] + [dev_a(k) for k in range(1, 8)] + [dev_b(k) for k in range(1, 8)]
    partners += [dev_x(k) for k in range(1, 4)]
    for who in partners:
        pl.semaphore_signal(barrier, inc=1, device_id=who, device_id_type=MESH)

    sends = []

    def send(src, dst, s_sem, r_sem, who):
        copy = pltpu.make_async_remote_copy(
            src_ref=src, dst_ref=dst, send_sem=s_sem, recv_sem=r_sem,
            device_id=who, device_id_type=MESH,
        )
        copy.start()
        sends.append(copy)
        return copy

    fetch[0].wait()
    fetch[1].wait()
    hid = jnp.concatenate(
        [hid_v[s].astype(F32) for s in range(STEPS)] + [jnp.zeros((SLOT - ROWS, hid_v.shape[2]), F32)],
        axis=0,
    ).astype(BF16)
    for h in range(HEADS):
        q_part[slot(h)] = jnp.dot(
            hid, wq_v[:, h * HD : (h + 1) * HD], preferred_element_type=F32
        )
    pl.semaphore_wait(barrier, len(partners))

    go = send(
        q_part.at[pl.ds(pl.multiple_of((HALF - mine) * SLOT, SLOT), HALF * SLOT)],
        q_core, core_s.at[0], core_r.at[0], sibling,
    )
    for one in fetch[2:7]:
        one.wait()

    list_rows[...] = jnp.full(list_rows.shape, -1, jnp.int32)
    for s in range(STEPS):
        for r in range(REQ):
            i = s * REQ + r
            list_rows[i : i + 1, :] = lists_v[s, r]
    nk_rows[...] = jnp.zeros(nk_rows.shape, F32)
    nv_rows[...] = jnp.zeros(nv_rows.shape, F32)
    for t in range(STEPS):
        for r in range(REQ):
            one_k = nk_v[t, r].astype(F32)
            one_v = nv_v[t, r].astype(F32)
            for s in range(t, STEPS):
                i = t * SLOT + s * REQ + r
                nk_rows[i : i + 1, :] = one_k
                nv_rows[i : i + 1, :] = one_v
    n_local = keys_v.shape[1] // BLK
    first = ctx * n_local
    lists = list_rows[...]
    for blk in range(n_local):
        hit = jnp.max(jnp.where(lists == first + blk, 1.0, 0.0), axis=1, keepdims=True)
        bias[:, blk * BLK : (blk + 1) * BLK] = jnp.broadcast_to(
            jnp.where(hit > 0.5, 0.0, NONE), (SLOT, BLK)
        )
    b_hi, b_mid, b_lo = split3(basis_v[0])
    for i, piece in enumerate((b_hi, b_mid, b_lo, b_hi, b_mid, b_hi)):
        rot[i * HD : (i + 1) * HD, :] = piece
    gain = gain_v[...].reshape(1, HD)

    go.wait_recv()
    q_half[...] = q_part[pl.ds(pl.multiple_of(mine * SLOT, SLOT), HALF * SLOT)] + q_core[...]
    got = [
        send(q_half.at[slot(ring_a(k))], q_rs.at[slot(k - 1)], rs_s.at[k - 1], rs_r.at[k - 1], dev_a(k))
        for k in range(1, 8)
    ]
    total = q_half[slot(a)]
    for k in range(1, 8):
        got[k - 1].wait_recv()
        total = total + q_rs[slot(k - 1)]
    q_own[slot(0)] = total
    got = [
        send(q_own.at[slot(0)], q_ex.at[slot(k - 1)], ex_s.at[k - 1], ex_r.at[k - 1], dev_b(k))
        for k in range(1, 8)
    ]
    for k in range(1, 8):
        got[k - 1].wait_recv()
        total = total + q_ex[slot(k - 1)]

    scale = HD ** (-0.5)
    norm = lax.rsqrt(jnp.mean(total * total, axis=1, keepdims=True) + 1e-06) * scale
    g_hi, g_mid, g_lo = split3(total * gain)
    turned = jnp.dot(
        jnp.concatenate([g_hi, g_hi, g_hi, g_mid, g_mid, g_lo], axis=1),
        rot[...],
        preferred_element_type=F32,
    )
    q_mine = turned * norm
    q_all[slot(mine + a)] = q_mine
    got = [
        send(
            q_all.at[slot(mine + a)], q_all.at[slot(mine + a)],
            ag_s.at[k - 1], ag_r.at[k - 1], dev_a(k),
        )
        for k in range(1, 8)
    ]
    for one in fetch[7:]:
        one.wait()
    for one in got:
        one.wait_recv()
    half = pl.ds(pl.multiple_of(mine * SLOT, SLOT), HALF * SLOT)
    go = send(q_all.at[half], q_all.at[half], core_s.at[1], core_r.at[1], sibling)
    go.wait_recv()

    lane48 = iota((STEPS * HEADS, HD), 1)
    lane16 = iota((HEADS, HD), 1)
    stat = jnp.zeros((HEADS, HD), F32)
    n_rows = STEPS * HEADS
    for r in range(REQ):
        q = jnp.concatenate(
            [q_all[pl.ds(s * REQ + r, HEADS, stride=SLOT), :] for s in range(STEPS)], axis=0
        )
        low = jnp.where(lane48 < RANK, q, 0.0)
        lhs = jnp.concatenate(split3(jnp.concatenate([q, low], axis=0)), axis=1)
        k_r = keys_v[r]
        scores = lax.dot_general(
            lhs, jnp.concatenate([k_r, k_r, k_r], axis=1), (((1,), (1,)), ((), ())),
            preferred_element_type=F32,
        )
        exact = jnp.concatenate(
            [
                scores[s * HEADS : (s + 1) * HEADS] + bias[s * REQ + r : s * REQ + r + 1, :]
                for s in range(STEPS)
            ],
            axis=0,
        )
        top = jnp.max(exact, axis=1, keepdims=True)
        probs = jnp.exp(exact - top)
        mass = jnp.sum(probs, axis=1, keepdims=True)
        acc = jnp.dot(probs.astype(BF16), vals_v[r], preferred_element_type=F32) / mass
        lse = top + jnp.log(mass)
        blocks = jnp.full((n_rows, HD), NONE, F32)
        for blk in range(n_local):
            part = scores[n_rows:, blk * BLK : (blk + 1) * BLK]
            peak = jnp.max(part, axis=1, keepdims=True)
            one = peak + jnp.log(jnp.sum(jnp.exp(part - peak), axis=1, keepdims=True))
            blocks = jnp.where(lane48 == blk, one, blocks)
        peak = jnp.max(blocks, axis=1, keepdims=True)
        low_lse = peak + jnp.log(jnp.sum(jnp.exp(blocks - peak), axis=1, keepdims=True))
        for s in range(STEPS):
            i = s * REQ + r
            rows = slice(s * HEADS, (s + 1) * HEADS)
            o_part[pl.ds(i, HEADS, stride=SLOT), :] = acc[rows]
            lse_all[slot(i)] = blocks[rows]
            stat = jnp.where(lane16 == i, lse[rows], stat)
            stat = jnp.where(lane16 == LOW + i, low_lse[rows], stat)
    o_part[pl.ds(STAT, HEADS, stride=SLOT), :] = stat
    for i in range(STAT + 1, SLOT):
        o_part[pl.ds(i, HEADS, stride=SLOT), :] = jnp.zeros((HEADS, HD), F32)

    go = send(
        o_part.at[pl.ds(pl.multiple_of((HALF - mine) * SLOT, SLOT), HALF * SLOT)],
        o_core, core_s.at[2], core_r.at[2], sibling,
    )
    row16 = iota((SLOT, 1), 0)
    fresh = [
        jnp.where(
            row16 >= t * REQ,
            jnp.sum(q_mine * nk_rows[slot(t)], axis=1, keepdims=True),
            NONE,
        )
        for t in range(STEPS)
    ]
    top = jnp.maximum(jnp.maximum(fresh[0], fresh[1]), fresh[2])
    new_w = [jnp.exp(f - top) for f in fresh]
    new_sum = new_w[0] + new_w[1] + new_w[2]
    new_o = sum(
        new_w[t].astype(BF16).astype(F32) * nv_rows[slot(t)] for t in range(STEPS)
    ) / new_sum
    diag = iota((SLOT, HD), 0) == iota((SLOT, HD), 1)
    new_row = jnp.sum(jnp.where(diag, top + jnp.log(new_sum), 0.0), axis=0, keepdims=True)
    new_row = jnp.where(iota((1, HD), 1) < ROWS, new_row, NONE)

    def is_stat():
        return iota((SLOT, HD), 0) == STAT

    go.wait_recv()
    mine_row = mine * SLOT
    stat0 = o_part[pl.ds(mine_row + STAT, HALF, stride=SLOT), :]
    stat1 = o_core[pl.ds(STAT, HALF, stride=SLOT), :]
    top = jnp.maximum(stat0, stat1)
    w0 = jnp.exp(stat0 - top)
    w1 = jnp.exp(stat1 - top)
    both = w0 + w1
    stat = top + jnp.log(both)
    w0 = w0 / both
    for h in range(HALF):
        f0 = column(w0[h : h + 1])
        o0 = o_part[slot(mine + h)]
        o1 = o_core[slot(h)]
        o_half[slot(h)] = jnp.where(is_stat(), stat[h : h + 1], o0 * f0 + o1 * (1.0 - f0))
    got = [
        send(o_half.at[slot(ring_a(k))], o_rs.at[slot(k - 1)], rs_s.at[6 + k], rs_r.at[6 + k], dev_a(k))
        for k in range(1, 8)
    ]

    def combine(parts):
        rows = [p[STAT : STAT + 1] if p.shape[0] == SLOT else p for p in parts]
        return rows

    def merge(outs, rows):
        top = rows[0]
        for one in rows[1:]:
            top = jnp.maximum(top, one)
        ws = [jnp.exp(one - top) for one in rows]
        total = sum(ws)
        inv = 1.0 / total
        res = sum(o * column(w * inv) for o, w in zip(outs, ws))
        return res, top + jnp.log(total)

    own = o_half[slot(a)]
    for one in got:
        one.wait_recv()
    outs = [own] + [o_rs[slot(k - 1)] for k in range(1, 8)]
    res, row = merge(outs, [p[STAT : STAT + 1] for p in outs])
    own = jnp.where(is_stat(), row, res)
    o_own[slot(0)] = own
    got = [
        send(o_own.at[slot(0)], o_ex.at[slot(k - 1)], ex_s.at[6 + k], ex_r.at[6 + k], dev_b(k))
        for k in range(1, 8)
    ]
    for one in got:
        one.wait_recv()
    outs = [own] + [o_ex[slot(k - 1)] for k in range(1, 8)]
    res, row = merge(outs + [new_o], [p[STAT : STAT + 1] for p in outs] + [new_row])
    o_all[slot(mine + a)] = jnp.where(is_stat(), row, res.astype(BF16).astype(F32))
    got = [
        send(
            o_all.at[slot(mine + a)], o_all.at[slot(mine + a)],
            ag_s.at[6 + k], ag_r.at[6 + k], dev_a(k),
        )
        for k in range(1, 8)
    ]
    for one in got:
        one.wait_recv()
    go = send(o_all.at[half], o_all.at[half], core_s.at[3], core_r.at[3], sibling)
    go.wait_recv()

    attn = jnp.concatenate([o_all[slot(h)].astype(BF16) for h in range(HEADS)], axis=1)
    term = jnp.dot(attn, wo_v[...], preferred_element_type=F32).astype(BF16).astype(F32)
    cols = term.shape[1]
    x_own[...] = jnp.zeros(x_own.shape, F32)
    x_own[:, :cols] = term
    got = [
        send(x_own, x_in.at[slot(k - 1)], x_s.at[k - 1], x_r.at[k - 1], dev_x(k))
        for k in range(1, 4)
    ]
    stat = o_all[pl.ds(STAT, HEADS, stride=SLOT), :]
    for s in range(STEPS):
        for r in range(REQ):
            i = s * REQ + r
            mass_o[s, r] = (lse_all[slot(i)] - stat[:, LOW + i : LOW + i + 1])[:, :n_local]
    for one in got:
        one.wait_recv()
    for k in range(1, 4):
        term = term + x_in[slot(k - 1), :cols]
    for s in range(STEPS):
        out_o[s] = term[s * REQ : (s + 1) * REQ].astype(BF16)
    for one in sends:
        one.wait_send()


def body(hidden, w_query, q_gain, basis, keys, values, new_keys, new_values, block_lists, w_out):
    n_tok = keys.shape[2]
    n_local = n_tok // BLK
    ops = (hidden, w_query, q_gain, basis, keys, values, new_keys, new_values, block_lists, w_out)
    slots = lambda n: pltpu.VMEM((n * SLOT, HD), F32)
    landing = [pltpu.VMEM(o.shape, o.dtype) for o in ops]
    landing[4] = landing[5] = pltpu.VMEM((REQ, n_tok, HD), BF16)
    dma = lambda n: pltpu.SemaphoreType.DMA((n,))

    def run(*refs):
        refs = list(refs)
        refs[4] = refs[4].at[:, 0]
        refs[5] = refs[5].at[:, 0]
        kernel(*refs)

    return pl.pallas_call(
        run,
        out_shape=(
            jax.ShapeDtypeStruct((STEPS, REQ, HEADS, n_local), F32),
            jax.ShapeDtypeStruct((STEPS, REQ, w_out.shape[1]), BF16),
        ),
        in_specs=[pl.BlockSpec(memory_space=pl.ANY)] * len(ops),
        out_specs=(pl.BlockSpec(memory_space=pltpu.VMEM),) * 2,
        scratch_shapes=landing
        + [
            pltpu.VMEM((SLOT, block_lists.shape[3]), jnp.int32),
            pltpu.VMEM((SLOT, n_tok), F32),
            slots(STEPS),
            slots(STEPS),
            pltpu.VMEM((6 * HD, HD), BF16),
        ]
        + [slots(n) for n in (16, 8, 8, 7, 1, 7, 16)]
        + [slots(n) for n in (16, 8, 8, 7, 1, 7, 16, 12)]
        + [slots(1), slots(3)]
        + [dma(n) for n in (10, 4, 4, 14, 14, 14, 14, 14, 14, 3, 3)],
        compiler_params=pltpu.CompilerParams(
            collective_id=0, has_side_effects=True, vmem_limit_bytes=48 * 2**20
        ),
        name="decode",
    )(*ops)


def solution(mesh):
    placed = (
        P(None, None, "ctx"),
        P("ctx", "kvh"),
        P(),
        P("kvh", None, None),
        P(None, "kvh", "ctx", None),
        P(None, "kvh", "ctx", None),
        P(None, None, "kvh", None),
        P(None, None, "kvh", None),
        P(None, None, "kvh", None),
        P("kvh", "ctx"),
    )
    return jax.shard_map(
        body,
        mesh=mesh,
        in_specs=placed,
        out_specs=(P(None, None, "kvh", "ctx"), P(None, None, "ctx")),
        check_vma=False,
    )
```

time: 935 us -> 70.2 us (0.08)
  blocking collectives: 494 us -> 0 us
  waiting for transfers between devices: 366 us -> 0 us
  Pallas kernels: 0 us -> 58.6 us
  other arithmetic: 24.4 us -> 0 us
  matrix products: 21 us -> 0 us
  between operations: 14.6 us -> 0.66 us
    pmax x1 -> x0, blocking collectives: 486 us -> none  [body(): glob_low, glob_exact = lax.pmax((low_top, exact_top), 'ctx')]
    psum x2 -> x0, waiting for transfers between devices: 366 us -> none  [the longest x1 186 us: body(): lax.psum((low_sum * jnp.exp(low_top - glob_low), exact_sum * shrink, acc...]
    pallas_call x0 -> x1, Pallas kernels: none -> 58.6 us  [body(): pl.pallas_call(run, out_shape=(jax.ShapeDtypeStruct((STEPS, REQ, HEADS, n...]
    dot_general x24 -> x0, matrix products: 21 us -> none  [the longest x3 5.09 us: body(): jnp.dot(hid_rows.reshape(n_rows * n_reqs, -1), w_query, preferred_element...]
  transfers between devices with their start and end apart: 2 -> 0, of which waited for: 2 -> 0; matrix products, arithmetic and copies ran while one was open for 1% -> 0% of each run, Pallas kernels for 0% -> 0%
where the time goes in v1:
time: 70.2 us; the launch traced here: 69.8 us
  Pallas kernels  58.6 us (83%)
  local copies, waits for them, and re-layouts  10.5 us (15%)
    pallas_call x1, Pallas kernels, body(): pl.pallas_call(run, out_shape=(jax.ShapeDtypeStruct((STEPS, REQ, HEADS, n...  58.6 us
    unnamed x18, local copies, waits for them, and re-layouts  9.73 us

profile of v1, /device:TPU:1, one launch (start us, length us, event | category | flops | bytes accessed | tf_op | source)
XLA Modules:
  0.0 69.8 jit_solution(150363312387497928)
XLA Ops:
  0.6 0.7 copy.12.refs_6_
  1.3 0.7 copy.13.refs_7_
  2.0 1.2 %copy.14.refs_9_ = bf16[2048,32]{1,0:T(8,128)(2,1)S(1)} copy(bf16[2048,32]{0,1:T(8,128)(2,1)} %param.19) | data formatting | bytes 262144 | tf_op args[9]
  3.2 0.0 copy-start
  3.2 1.4 %copy-done = bf16[4,1,1536,128]{3,2,1,0:T(8,128)(2,1)S(1)} copy-done((bf16[4,1,1536,128]{3,2,1,0:T(8,128)(2,1)S(1)}, bf16[4,1,1536,128]{3,2,1,0:T(8,128)(2,1)}, u32[]{:S(2)}) %copy-start) | copy-done | bytes 1572888
  4.6 0.0 copy-start.1
  4.6 1.4 %copy-done.1 = bf16[4,1,1536,128]{3,2,1,0:T(8,128)(2,1)S(1)} copy-done((bf16[4,1,1536,128]{3,2,1,0:T(8,128)(2,1)S(1)}, bf16[4,1,1536,128]{3,2,1,0:T(8,128)(2,1)}, u32[]{:S(2)}) %copy-start.1) | copy-done | bytes 1572888
  6.0 0.0 copy-start.2
  6.0 0.9 %copy-done.2 = bf16[32,2048]{1,0:T(8,128)(2,1)S(1)} copy-done((bf16[32,2048]{1,0:T(8,128)(2,1)S(1)}, bf16[32,2048]{1,0:T(8,128)(2,1)}, u32[]{:S(2)}) %copy-start.2) | copy-done | bytes 131096
  6.9 0.0 copy-start.3
  6.9 0.8 %copy-done.3 = f32[1,128,128]{2,1,0:T(8,128)S(1)} copy-done((f32[1,128,128]{2,1,0:T(8,128)S(1)}, f32[1,128,128]{2,1,0:T(8,128)}, u32[]{:S(2)}) %copy-start.3) | copy-done | bytes 65560
  7.8 0.0 copy-start.4
  7.8 0.7 %copy-done.4 = s32[3,4,1,256]{3,2,1,0:T(1,128)S(1)} copy-done((s32[3,4,1,256]{3,2,1,0:T(1,128)S(1)}, s32[3,4,1,256]{3,2,1,0:T(1,128)}, u32[]{:S(2)}) %copy-start.4) | copy-done | bytes 12312
  8.5 0.0 copy-start.5
  8.5 0.7 copy-done.5
  9.2 0.0 copy-start.6
  9.2 0.7 copy-done.6
  9.8 58.6 %decode.1 = (f32[3,4,16,12]{3,2,1,0:T(8,128)S(1)}, bf16[3,4,32]{2,1,0:T(4,128)(2,1)S(1)}) custom-call(bf16[3,4,32]{2,1,0:T(4,128)(2,1)S(1)} %copy-done.5, bf16[32,2048]{1,0:T(8,128)(2,1)S(1)} %copy-done.2, f32[128]{0:T(128)S(1)} %copy-done.6, f32[1,128,128]{2,1,0:T(8,128)S(1)} %copy-done.3, bf16[4,1,1536,128]{3,2,1,0:T(8,128)(2,1)S(1)} %copy-done, ...), custom_call_target="tpu_custom_call" | custom-call | tf_op jit(solution)/shard_map/decode/pallas_call | solution.py:377
  68.4 0.8 %copy.15 = f32[3,4,16,12]{2,1,3,0:T(4,128)} copy(f32[3,4,16,12]{3,2,1,0:T(8,128)S(1)} %get-tuple-element.2) | data formatting | bytes 18432 | tf_op jit(solution)/shard_map/decode/pallas_call | solution.py:377
  69.2 0.6 copy.17
Async XLA Ops:
  3.2 1.4 %copy-start = (bf16[4,1,1536,128]{3,2,1,0:T(8,128)(2,1)S(1)}, bf16[4,1,1536,128]{3,2,1,0:T(8,128)(2,1)}, u32[]{:S(2)}) copy-start(bf16[4,1,1536,128]{3,2,1,0:T(8,128)(2,1)} %refs_4_.1) | copy-start | bytes 4718596
  4.6 1.4 %copy-start.1 = (bf16[4,1,1536,128]{3,2,1,0:T(8,128)(2,1)S(1)}, bf16[4,1,1536,128]{3,2,1,0:T(8,128)(2,1)}, u32[]{:S(2)}) copy-start(bf16[4,1,1536,128]{3,2,1,0:T(8,128)(2,1)} %refs_5_.1) | copy-start | bytes 4718596
  6.0 0.9 %copy-start.2 = (bf16[32,2048]{1,0:T(8,128)(2,1)S(1)}, bf16[32,2048]{1,0:T(8,128)(2,1)}, u32[]{:S(2)}) copy-start(bf16[32,2048]{1,0:T(8,128)(2,1)} %refs_1_.1) | copy-start | bytes 393220
  6.9 0.8 %copy-start.3 = (f32[1,128,128]{2,1,0:T(8,128)S(1)}, f32[1,128,128]{2,1,0:T(8,128)}, u32[]{:S(2)}) copy-start(f32[1,128,128]{2,1,0:T(8,128)} %refs_3_.1) | copy-start | bytes 196612
  7.8 0.7 %copy-start.4 = (s32[3,4,1,256]{3,2,1,0:T(1,128)S(1)}, s32[3,4,1,256]{3,2,1,0:T(1,128)}, u32[]{:S(2)}) copy-start(s32[3,4,1,256]{3,2,1,0:T(1,128)} %refs_8_.1) | copy-start | bytes 36868
  8.5 0.7 copy-start.5
  9.2 0.7 copy-start.6

commit v2 on v1

v2 whole, which is shorter than its diff:
```python
import jax
import jax.numpy as jnp
from jax import lax
from jax.experimental import pallas as pl
from jax.experimental.pallas import tpu as pltpu
from jax.sharding import PartitionSpec as P

RANK = 32
BLK = 128
STEPS = 3
REQ = 4
ROWS = STEPS * REQ
SLOT = 16
STAT = 12
LOW = 16
HEADS = 16
HALF = 8
HD = 128
NONE = -1e30
FAR_FIRST = (4, 3, 5, 2, 6, 1, 7)
MESH = pl.DeviceIdType.MESH
F32 = jnp.float32
BF16 = jnp.bfloat16


def split3(x):
    hi = x.astype(BF16)
    rest = x - hi.astype(F32)
    mid = rest.astype(BF16)
    lo = (rest - mid.astype(F32)).astype(BF16)
    return hi, mid, lo


def slot(i):
    if isinstance(i, int):
        return pl.ds(i * SLOT, SLOT)
    return pl.ds(pl.multiple_of(i * SLOT, SLOT), SLOT)


def rows_of(i):
    if isinstance(i, int):
        return pl.ds(i * SLOT, ROWS)
    return pl.ds(pl.multiple_of(i * SLOT, SLOT), ROWS)


def iota(shape, dim):
    return lax.broadcasted_iota(jnp.int32, shape, dim)


def column(row):
    diag = iota((SLOT, HD), 0) == iota((SLOT, HD), 1)
    return jnp.sum(jnp.where(diag, row, 0.0), axis=1, keepdims=True)


def stat_of(x):
    return x[STAT : STAT + 1] + x[STAT + 1 : STAT + 2] + x[STAT + 2 : STAT + 3]


def with_stat(x, row):
    i = iota((SLOT, HD), 0)
    hi, mid, lo = (p.astype(F32) for p in split3(row))
    tail = jnp.where(i == STAT, hi, jnp.where(i == STAT + 1, mid, lo))
    return jnp.where(i < ROWS, x, jnp.where(i < STAT + 3, tail, 0.0)).astype(BF16)


def merge(outs, rows):
    top = rows[0]
    for one in rows[1:]:
        top = jnp.maximum(top, one)
    ws = [jnp.exp(one - top) for one in rows]
    total = sum(ws)
    inv = 1.0 / total
    res = sum(o * column(w * inv) for o, w in zip(outs, ws))
    return res, top + jnp.log(total)


def kernel(
    hid_h, wq_h, gain_h, basis_h, keys_h, vals_h, nk_h, nv_h, lists_h, wo_h,
    mass_o, out_o,
    hid_v, wq_v, gain_v, basis_v, keys_v, vals_v, nk_v, nv_v, lists_v, wo_v,
    list_rows, bias, nk_rows, nv_rows, rot, wo_t,
    q_part, q_rs, q_own, q_ex, q_all,
    o_wide, lse_all,
    o_part, o_rs, o_own, o_ex, o_all, x_own, x_in,
    in_sem, rs_s, rs_r, ex_s, ex_r, ag_s, ag_r, x_s, x_r,
):
    ctx = lax.axis_index("ctx")
    x = lax.axis_index("kvh")
    y = ctx // 16
    z = lax.rem(ctx // 2, 8)
    c = lax.rem(ctx, 2)
    a = z + c * (y - z)
    b = y + c * (z - y)
    mine = c * HALF + a
    theirs = (1 - c) * HALF

    def at(aa, bb, cc):
        yy = bb + c * (aa - bb)
        zz = aa + c * (bb - aa)
        return ((yy * 8 + zz) * 2 + cc, x)

    def ring_a(k):
        return lax.rem(a + k, HALF)

    def ring_b(k):
        return lax.rem(b + k, HALF)

    def dev_a(k):
        return at(ring_a(k), b, c)

    def dev_b(k):
        return at(a, ring_b(k), c)

    def cross_a(k):
        return at(ring_a(k), b, 1 - c)

    def cross_b(k):
        return at(a, ring_b(k), 1 - c)

    def dev_x(k):
        return (ctx, lax.rem(x + k, 4))

    pairs = (
        (hid_h, hid_v), (wq_h, wq_v), (gain_h, gain_v), (basis_h, basis_v), (lists_h, lists_v),
        (nk_h, nk_v), (nv_h, nv_v), (wo_h, wo_v), (keys_h, keys_v), (vals_h, vals_v),
    )
    fetch = [pltpu.make_async_copy(s, d, in_sem.at[i]) for i, (s, d) in enumerate(pairs)]
    for one in fetch:
        one.start()
    barrier = pltpu.get_barrier_semaphore()
    partners = []
    for k in FAR_FIRST:
        partners += [dev_a(k), dev_b(k), cross_a(k), cross_b(k)]
    partners += [dev_x(2), dev_x(1), dev_x(3), cross_a(0)]
    for who in partners:
        pl.semaphore_signal(barrier, inc=1, device_id=who, device_id_type=MESH)

    sends = []

    def send(src, dst, s_sem, r_sem, who):
        copy = pltpu.make_async_remote_copy(
            src_ref=src, dst_ref=dst, send_sem=s_sem, recv_sem=r_sem,
            device_id=who, device_id_type=MESH,
        )
        copy.start()
        sends.append(copy)
        return copy

    def scatter(part, into, cut, base):
        got = {}
        for k in FAR_FIRST + (0,):
            if k:
                got[k - 1] = send(
                    part.at[cut(c * HALF + ring_a(k))], into.at[cut(k - 1)],
                    rs_s.at[base + k - 1], rs_r.at[base + k - 1], dev_a(k),
                )
            got[7 + k] = send(
                part.at[cut(theirs + ring_b(k))], into.at[cut(7 + k)],
                rs_s.at[base + 7 + k], rs_r.at[base + 7 + k], cross_b(k),
            )
        return [got[i] for i in range(15)]

    def gather(buf, cut, base):
        got = {}
        for k in FAR_FIRST + (0,):
            if k:
                got[k - 1] = send(
                    buf.at[cut(mine)], buf.at[cut(mine)],
                    ag_s.at[base + k - 1], ag_r.at[base + k - 1], dev_a(k),
                )
            got[7 + k] = send(
                buf.at[cut(mine)], buf.at[cut(mine)],
                ag_s.at[base + 7 + k], ag_r.at[base + 7 + k], cross_a(k),
            )
        return [got[i] for i in range(15)]

    def exchange(own, into, cut, base):
        got = {}
        for k in FAR_FIRST:
            got[k - 1] = send(
                own.at[cut(0)], into.at[cut(k - 1)],
                ex_s.at[base + k - 1], ex_r.at[base + k - 1], dev_b(k),
            )
        return [got[i] for i in range(7)]

    fetch[0].wait()
    fetch[1].wait()
    hid = jnp.concatenate(
        [hid_v[s].astype(F32) for s in range(STEPS)] + [jnp.zeros((SLOT - ROWS, hid_v.shape[2]), F32)],
        axis=0,
    ).astype(BF16)
    for h in range(HEADS):
        q_part[slot(h)] = jnp.dot(
            hid, wq_v[:, h * HD : (h + 1) * HD], preferred_element_type=F32
        )
    pl.semaphore_wait(barrier, len(partners))

    got = scatter(q_part, q_rs, rows_of, 0)
    for one in fetch[2:8]:
        one.wait()

    list_rows[...] = jnp.full(list_rows.shape, -1, jnp.int32)
    for s in range(STEPS):
        for r in range(REQ):
            i = s * REQ + r
            list_rows[i : i + 1, :] = lists_v[s, r]
    nk_rows[...] = jnp.zeros(nk_rows.shape, F32)
    nv_rows[...] = jnp.zeros(nv_rows.shape, F32)
    for t in range(STEPS):
        one_k = nk_v[t].astype(F32)
        one_v = nv_v[t].astype(F32)
        for s in range(t, STEPS):
            i = t * SLOT + s * REQ
            nk_rows[i : i + REQ, :] = one_k
            nv_rows[i : i + REQ, :] = one_v
    n_local = keys_v.shape[1] // BLK
    first = ctx * n_local
    lists = list_rows[...]
    for blk in range(n_local):
        hit = jnp.max(jnp.where(lists == first + blk, 1.0, 0.0), axis=1, keepdims=True)
        bias[:, blk * BLK : (blk + 1) * BLK] = jnp.broadcast_to(
            jnp.where(hit > 0.5, 0.0, NONE), (SLOT, BLK)
        )
    b_hi, b_mid, b_lo = split3(basis_v[0])
    for i, piece in enumerate((b_hi, b_mid, b_lo, b_hi, b_mid, b_hi)):
        rot[i * HD : (i + 1) * HD, :] = piece
    gain = gain_v[...].reshape(1, HD)
    wo_t[...] = wo_v[...].astype(F32).T.astype(BF16)

    total = q_part[slot(mine)]
    for k in range(15):
        got[k].wait_recv()
        total = total + q_rs[slot(k)]
    total = jnp.where(iota((SLOT, HD), 0) < ROWS, total, 0.0)
    q_own[...] = total
    got = exchange(q_own, q_ex, rows_of, 0)
    for k in range(7):
        got[k].wait_recv()
        total = total + q_ex[slot(k)]
    total = jnp.where(iota((SLOT, HD), 0) < ROWS, total, 0.0)

    scale = HD ** (-0.5)
    norm = lax.rsqrt(jnp.mean(total * total, axis=1, keepdims=True) + 1e-06) * scale
    g_hi, g_mid, g_lo = split3(total * gain)
    turned = jnp.dot(
        jnp.concatenate([g_hi, g_hi, g_hi, g_mid, g_mid, g_lo], axis=1),
        rot[...],
        preferred_element_type=F32,
    )
    q_mine = turned * norm
    q_all[slot(mine)] = q_mine
    got = gather(q_all, rows_of, 0)
    for one in fetch[8:]:
        one.wait()
    for one in got:
        one.wait_recv()

    lane48 = iota((STEPS * HEADS, HD), 1)
    lane16 = iota((HEADS, HD), 1)
    stat = jnp.zeros((HEADS, HD), F32)
    n_rows = STEPS * HEADS
    for r in range(REQ):
        q = jnp.concatenate(
            [q_all[pl.ds(s * REQ + r, HEADS, stride=SLOT), :] for s in range(STEPS)], axis=0
        )
        low = jnp.where(lane48 < RANK, q, 0.0)
        lhs = jnp.concatenate(split3(jnp.concatenate([q, low], axis=0)), axis=1)
        k_r = keys_v[r]
        scores = lax.dot_general(
            lhs, jnp.concatenate([k_r, k_r, k_r], axis=1), (((1,), (1,)), ((), ())),
            preferred_element_type=F32,
        )
        exact = jnp.concatenate(
            [
                scores[s * HEADS : (s + 1) * HEADS] + bias[s * REQ + r : s * REQ + r + 1, :]
                for s in range(STEPS)
            ],
            axis=0,
        )
        top = jnp.max(exact, axis=1, keepdims=True)
        probs = jnp.exp(exact - top)
        mass = jnp.sum(probs, axis=1, keepdims=True)
        acc = jnp.dot(probs.astype(BF16), vals_v[r], preferred_element_type=F32) / mass
        lse = top + jnp.log(mass)
        blocks = jnp.full((n_rows, HD), NONE, F32)
        for blk in range(n_local):
            part = scores[n_rows:, blk * BLK : (blk + 1) * BLK]
            peak = jnp.max(part, axis=1, keepdims=True)
            one = peak + jnp.log(jnp.sum(jnp.exp(part - peak), axis=1, keepdims=True))
            blocks = jnp.where(lane48 == blk, one, blocks)
        peak = jnp.max(blocks, axis=1, keepdims=True)
        low_lse = peak + jnp.log(jnp.sum(jnp.exp(blocks - peak), axis=1, keepdims=True))
        for s in range(STEPS):
            i = s * REQ + r
            rows = slice(s * HEADS, (s + 1) * HEADS)
            o_wide[pl.ds(i, HEADS, stride=SLOT), :] = acc[rows]
            lse_all[slot(i)] = blocks[rows]
            stat = jnp.where(lane16 == i, lse[rows], stat)
            stat = jnp.where(lane16 == LOW + i, low_lse[rows], stat)
    for i, piece in enumerate(split3(stat)):
        o_wide[pl.ds(STAT + i, HEADS, stride=SLOT), :] = piece.astype(F32)
    o_wide[pl.ds(SLOT - 1, HEADS, stride=SLOT), :] = jnp.zeros((HEADS, HD), F32)
    o_part[...] = o_wide[...].astype(BF16)

    got = scatter(o_part, o_rs, slot, 15)
    row16 = iota((SLOT, 1), 0)
    fresh = [
        jnp.where(
            row16 >= t * REQ,
            jnp.sum(q_mine * nk_rows[slot(t)], axis=1, keepdims=True),
            NONE,
        )
        for t in range(STEPS)
    ]
    top = jnp.maximum(jnp.maximum(fresh[0], fresh[1]), fresh[2])
    new_w = [jnp.exp(f - top) for f in fresh]
    new_sum = new_w[0] + new_w[1] + new_w[2]
    new_o = sum(
        new_w[t].astype(BF16).astype(F32) * nv_rows[slot(t)] for t in range(STEPS)
    ) / new_sum
    diag = iota((SLOT, HD), 0) == iota((SLOT, HD), 1)
    new_row = jnp.sum(jnp.where(diag, top + jnp.log(new_sum), 0.0), axis=0, keepdims=True)
    new_row = jnp.where(iota((1, HD), 1) < ROWS, new_row, NONE)

    for one in got:
        one.wait_recv()
    outs = [o_wide[slot(mine)]] + [o_rs[slot(k)].astype(F32) for k in range(15)]
    res, row = merge(outs, [stat_of(p) for p in outs])
    o_own[...] = with_stat(res, row)
    got = exchange(o_own, o_ex, slot, 7)
    for one in got:
        one.wait_recv()
    outs = [o_ex[slot(k)].astype(F32) for k in range(7)]
    res, row = merge([res, new_o] + outs, [row, new_row] + [stat_of(p) for p in outs])
    o_all[slot(mine)] = with_stat(res, row)
    got = gather(o_all, slot, 15)
    for one in got:
        one.wait_recv()

    attn = jnp.concatenate([o_all[slot(h)] for h in range(HEADS)], axis=1)
    term = jnp.dot(attn, wo_t[...], preferred_element_type=F32).astype(BF16)
    cols = term.shape[1]
    x_own[:, :cols] = term
    got = [
        send(x_own, x_in.at[slot(k - 1)], x_s.at[k - 1], x_r.at[k - 1], dev_x(k))
        for k in (2, 1, 3)
    ]
    o_wide[...] = o_all[...].astype(F32)
    stat = sum(o_wide[pl.ds(STAT + i, HEADS, stride=SLOT), :] for i in range(3))
    for s in range(STEPS):
        for r in range(REQ):
            i = s * REQ + r
            mass_o[s, r] = (lse_all[slot(i)] - stat[:, LOW + i : LOW + i + 1])[:, :n_local]
    for one in got:
        one.wait_recv()
    term = term.astype(F32)
    for k in range(1, 4):
        term = term + x_in[slot(k - 1), :cols].astype(F32)
    for s in range(STEPS):
        out_o[s] = term[s * REQ : (s + 1) * REQ].astype(BF16)
    for one in sends:
        one.wait_send()


def body(hidden, w_query, q_gain, basis, keys, values, new_keys, new_values, block_lists, w_out):
    n_tok = keys.shape[2]
    n_local = n_tok // BLK
    new_keys, new_values = new_keys[:, :, 0], new_values[:, :, 0]
    ops = (hidden, w_query, q_gain, basis, keys, values, new_keys, new_values, block_lists, w_out.T)
    slots = lambda n, kind=F32: pltpu.VMEM((n * SLOT, HD), kind)
    landing = [pltpu.VMEM(o.shape, o.dtype) for o in ops]
    landing[4] = landing[5] = pltpu.VMEM((REQ, n_tok, HD), BF16)
    dma = lambda n: pltpu.SemaphoreType.DMA((n,))

    def run(*refs):
        refs = list(refs)
        refs[4] = refs[4].at[:, 0]
        refs[5] = refs[5].at[:, 0]
        kernel(*refs)

    return pl.pallas_call(
        run,
        out_shape=(
            jax.ShapeDtypeStruct((STEPS, REQ, HEADS, n_local), F32),
            jax.ShapeDtypeStruct((STEPS, REQ, w_out.shape[1]), BF16),
        ),
        in_specs=[pl.BlockSpec(memory_space=pltpu.HBM)] * len(ops),
        out_specs=(pl.BlockSpec(memory_space=pltpu.VMEM),) * 2,
        scratch_shapes=landing
        + [
            pltpu.VMEM((SLOT, block_lists.shape[3]), jnp.int32),
            pltpu.VMEM((SLOT, n_tok), F32),
            slots(STEPS),
            slots(STEPS),
            pltpu.VMEM((6 * HD, HD), BF16),
            pltpu.VMEM((w_out.shape[0], w_out.shape[1]), BF16),
        ]
        + [slots(n) for n in (16, 15, 1, 7, 16, 16, 12)]
        + [slots(n, BF16) for n in (16, 15, 1, 7, 16, 1, 3)]
        + [dma(n) for n in (10, 30, 30, 14, 14, 30, 30, 3, 3)],
        compiler_params=pltpu.CompilerParams(
            collective_id=0, has_side_effects=True, vmem_limit_bytes=60 * 2**20
        ),
        name="decode",
    )(*ops)


def solution(mesh):
    placed = (
        P(None, None, "ctx"),
        P("ctx", "kvh"),
        P(),
        P("kvh", None, None),
        P(None, "kvh", "ctx", None),
        P(None, "kvh", "ctx", None),
        P(None, None, "kvh", None),
        P(None, None, "kvh", None),
        P(None, None, "kvh", None),
        P("kvh", "ctx"),
    )
    return jax.shard_map(
        body,
        mesh=mesh,
        in_specs=placed,
        out_specs=(P(None, None, "kvh", "ctx"), P(None, None, "ctx")),
        check_vma=False,
    )
```

time: 70.2 us -> 56.8 us (0.81)
  local copies, waits for them, and re-layouts: 10.5 us -> 2.93 us
  Pallas kernels: 58.6 us -> 53 us
    unnamed x18 -> x1, local copies, waits for them, and re-layouts: 9.73 us -> 1.26 us
    pallas_call x1, Pallas kernels: 58.6 us -> 53 us  [body(): pl.pallas_call(run, out_shape=(jax.ShapeDtypeStruct((STEPS, REQ, HEADS, n...]
    pallas_call x1, local copies, waits for them, and re-layouts: 0.78 us -> 1.67 us  [body(): pl.pallas_call(run, out_shape=(jax.ShapeDtypeStruct((STEPS, REQ, HEADS, n...]
where the time goes in v2:
time: 56.8 us; the launch traced here: 56.6 us
  Pallas kernels  53 us (93%)
  local copies, waits for them, and re-layouts  2.93 us (5%)
  between operations  0.64 us (1%)
    pallas_call x1, Pallas kernels, body(): pl.pallas_call(run, out_shape=(jax.ShapeDtypeStruct((STEPS, REQ, HEADS, n...  53 us
    pallas_call x1, local copies, waits for them, and re-layouts, body(): pl.pallas_call(run, out_shape=(jax.ShapeDtypeStruct((STEPS, REQ, HEADS, n...  1.67 us
    unnamed x1, local copies, waits for them, and re-layouts  1.26 us

profile of v2, /device:TPU:1, one launch (start us, length us, event | category | flops | bytes accessed | tf_op | source)
XLA Modules:
  0.0 56.6 jit_solution(9120662691920489522)
XLA Ops:
  0.6 53.0 %decode.1 = (f32[3,4,16,12]{3,2,1,0:T(8,128)}, bf16[3,4,32]{2,1,0:T(4,128)(2,1)}) custom-call(bf16[3,4,32]{2,1,0:T(4,128)(2,1)} %refs_0_.1, bf16[32,2048]{1,0:T(8,128)(2,1)} %refs_1_.1, f32[128]{0:T(128)} %refs_2_.1, f32[1,128,128]{2,1,0:T(8,128)} %refs_3_.1, bf16[4,1,1536,128]{3,2,1,0:T(8,128)(2,1)} %refs_4_.1, bf16[4,1,1536,128]{3,2,1,0:T(8,128)(2,1)} %refs_5_.1, ...), custom_call_target="tpu_custom_call" | custom-call | tf_op jit(solution)/shard_map/decode/pallas_call | solution.py:381
  53.7 1.7 %copy.12 = f32[3,4,16,12]{2,1,3,0:T(4,128)} copy(f32[3,4,16,12]{3,2,1,0:T(8,128)} %get-tuple-element.2) | data formatting | bytes 18432 | tf_op jit(solution)/shard_map/decode/pallas_call | solution.py:381
  55.3 1.3 %copy.14 = bf16[3,4,32]{2,1,0:T(4,128)(2,1)} copy(bf16[3,4,32]{2,1,0:T(4,128)(2,1)} %get-tuple-element.7) | data formatting | bytes 1536

commit v3 on v2

--- a/solution.py
+++ b/solution.py
@@ -78,11 +78,11 @@
     hid_h, wq_h, gain_h, basis_h, keys_h, vals_h, nk_h, nv_h, lists_h, wo_h,
     mass_o, out_o,
     hid_v, wq_v, gain_v, basis_v, keys_v, vals_v, nk_v, nv_v, lists_v, wo_v,
-    list_rows, bias, nk_rows, nv_rows, rot, wo_t,
+    list_rows, bias, nk_rows, nv_rows, rot, wo_t, keys_t, low_keys, mass_v, out_v,
     q_part, q_rs, q_own, q_ex, q_all,
     o_wide, lse_all,
     o_part, o_rs, o_own, o_ex, o_all, x_own, x_in,
-    in_sem, rs_s, rs_r, ex_s, ex_r, ag_s, ag_r, x_s, x_r,
+    in_sem, out_sem, rs_s, rs_r, ex_s, ex_r, ag_s, ag_r, x_s, x_r,
 ):
     ctx = lax.axis_index("ctx")
     x = lax.axis_index("kvh")
@@ -120,6 +120,13 @@
     def dev_x(k):
         return (ctx, lax.rem(x + k, 4))
 
+    barrier = pltpu.get_barrier_semaphore()
+    partners = []
+    for k in FAR_FIRST:
+        partners += [dev_a(k), dev_b(k), cross_a(k), cross_b(k)]
+    partners += [dev_x(2), dev_x(1), dev_x(3), cross_a(0)]
+    for who in partners:
+        pl.semaphore_signal(barrier, inc=1, device_id=who, device_id_type=MESH)
     pairs = (
         (hid_h, hid_v), (wq_h, wq_v), (gain_h, gain_v), (basis_h, basis_v), (lists_h, lists_v),
         (nk_h, nk_v), (nv_h, nv_v), (wo_h, wo_v), (keys_h, keys_v), (vals_h, vals_v),
@@ -127,13 +134,6 @@
     fetch = [pltpu.make_async_copy(s, d, in_sem.at[i]) for i, (s, d) in enumerate(pairs)]
     for one in fetch:
         one.start()
-    barrier = pltpu.get_barrier_semaphore()
-    partners = []
-    for k in FAR_FIRST:
-        partners += [dev_a(k), dev_b(k), cross_a(k), cross_b(k)]
-    partners += [dev_x(2), dev_x(1), dev_x(3), cross_a(0)]
-    for who in partners:
-        pl.semaphore_signal(barrier, inc=1, device_id=who, device_id_type=MESH)
 
     sends = []
 
@@ -196,7 +196,7 @@
     pl.semaphore_wait(barrier, len(partners))
 
     got = scatter(q_part, q_rs, rows_of, 0)
-    for one in fetch[2:8]:
+    for one in fetch[2:9]:
         one.wait()
 
     list_rows[...] = jnp.full(list_rows.shape, -1, jnp.int32)
@@ -226,6 +226,8 @@
         rot[i * HD : (i + 1) * HD, :] = piece
     gain = gain_v[...].reshape(1, HD)
     wo_t[...] = wo_v[...].astype(F32).T.astype(BF16)
+    for r in range(REQ):
+        keys_t[r] = keys_v[r].T
 
     total = q_part[slot(mine)]
     for k in range(15):
@@ -234,6 +236,11 @@
     total = jnp.where(iota((SLOT, HD), 0) < ROWS, total, 0.0)
     q_own[...] = total
     got = exchange(q_own, q_ex, rows_of, 0)
+    copies = (iota((HD, HD), 0) == lax.rem(iota((HD, HD), 1), RANK)).astype(F32).astype(BF16)
+    for r in range(REQ):
+        low_keys[r // 2, :, (r % 2) * HD : (r % 2 + 1) * HD] = jnp.dot(
+            keys_v[r], copies, preferred_element_type=F32
+        ).astype(BF16)
     for k in range(7):
         got[k].wait_recv()
         total = total + q_ex[slot(k)]
@@ -250,26 +257,25 @@
     q_mine = turned * norm
     q_all[slot(mine)] = q_mine
     got = gather(q_all, rows_of, 0)
-    for one in fetch[8:]:
-        one.wait()
+    fetch[9].wait()
     for one in got:
         one.wait_recv()
 
-    lane48 = iota((STEPS * HEADS, HD), 1)
     lane16 = iota((HEADS, HD), 1)
     stat = jnp.zeros((HEADS, HD), F32)
     n_rows = STEPS * HEADS
+    q_of = [
+        jnp.concatenate(
+            [q_all[pl.ds(s * REQ + r, HEADS, stride=SLOT), :] for s in range(STEPS)], axis=0
+        )
+        for r in range(REQ)
+    ]
+    parts_of = [split3(q) for q in q_of]
     for r in range(REQ):
-        q = jnp.concatenate(
-            [q_all[pl.ds(s * REQ + r, HEADS, stride=SLOT), :] for s in range(STEPS)], axis=0
-        )
-        low = jnp.where(lane48 < RANK, q, 0.0)
-        lhs = jnp.concatenate(split3(jnp.concatenate([q, low], axis=0)), axis=1)
-        k_r = keys_v[r]
-        scores = lax.dot_general(
-            lhs, jnp.concatenate([k_r, k_r, k_r], axis=1), (((1,), (1,)), ((), ())),
-            preferred_element_type=F32,
-        )
+        scores = jnp.dot(
+            jnp.concatenate(parts_of[r], axis=0), keys_t[r], preferred_element_type=F32
+        )
+        scores = scores[:n_rows] + scores[n_rows : 2 * n_rows] + scores[2 * n_rows :]
         exact = jnp.concatenate(
             [
                 scores[s * HEADS : (s + 1) * HEADS] + bias[s * REQ + r : s * REQ + r + 1, :]
@@ -282,21 +288,49 @@
         mass = jnp.sum(probs, axis=1, keepdims=True)
         acc = jnp.dot(probs.astype(BF16), vals_v[r], preferred_element_type=F32) / mass
         lse = top + jnp.log(mass)
-        blocks = jnp.full((n_rows, HD), NONE, F32)
-        for blk in range(n_local):
-            part = scores[n_rows:, blk * BLK : (blk + 1) * BLK]
-            peak = jnp.max(part, axis=1, keepdims=True)
-            one = peak + jnp.log(jnp.sum(jnp.exp(part - peak), axis=1, keepdims=True))
-            blocks = jnp.where(lane48 == blk, one, blocks)
-        peak = jnp.max(blocks, axis=1, keepdims=True)
-        low_lse = peak + jnp.log(jnp.sum(jnp.exp(blocks - peak), axis=1, keepdims=True))
         for s in range(STEPS):
             i = s * REQ + r
             rows = slice(s * HEADS, (s + 1) * HEADS)
             o_wide[pl.ds(i, HEADS, stride=SLOT), :] = acc[rows]
-            lse_all[slot(i)] = blocks[rows]
             stat = jnp.where(lane16 == i, lse[rows], stat)
-            stat = jnp.where(lane16 == LOW + i, low_lse[rows], stat)
+    lane48 = iota((n_rows, HD), 1)
+    for pair in range(REQ // 2):
+        sides = []
+        for half in range(2):
+            hi, mid, lo = (p.astype(F32) for p in parts_of[2 * pair + half])
+            packed = jnp.where(
+                lane48 < RANK,
+                hi,
+                jnp.where(
+                    lane48 < 2 * RANK,
+                    pltpu.roll(mid, RANK, 1),
+                    jnp.where(lane48 < 3 * RANK, pltpu.roll(lo, 2 * RANK, 1), 0.0),
+                ),
+            )
+            blank = jnp.zeros((HD // 2, HD), F32)
+            packed = jnp.concatenate([packed, blank[: HD // 2 - n_rows]], axis=0)
+            sides.append(jnp.concatenate([blank, packed] if half else [packed, blank], axis=0).T)
+        columns = jnp.concatenate(sides, axis=0).astype(BF16)
+        rows = []
+        for blk in range(n_local):
+            part = jnp.dot(
+                low_keys[pair, blk * BLK : (blk + 1) * BLK], columns, preferred_element_type=F32
+            )
+            peak = jnp.max(part, axis=0, keepdims=True)
+            rows.append(peak + jnp.log(jnp.sum(jnp.exp(part - peak), axis=0, keepdims=True)))
+        blocks = jnp.concatenate(rows, axis=0)
+        peak = jnp.max(blocks, axis=0, keepdims=True)
+        low_lse = peak + jnp.log(jnp.sum(jnp.exp(blocks - peak), axis=0, keepdims=True))
+        lse_all[pair, :n_local] = blocks
+        low_lse = jnp.broadcast_to(low_lse, (8, HD)).T
+        for half in range(2):
+            for s in range(STEPS):
+                at_row = half * (HD // 2) + s * HEADS
+                stat = jnp.where(
+                    lane16 == LOW + s * REQ + 2 * pair + half,
+                    low_lse[at_row : at_row + HEADS, :1],
+                    stat,
+                )
     for i, piece in enumerate(split3(stat)):
         o_wide[pl.ds(STAT + i, HEADS, stride=SLOT), :] = piece.astype(F32)
     o_wide[pl.ds(SLOT - 1, HEADS, stride=SLOT), :] = jnp.zeros((HEADS, HD), F32)
@@ -347,19 +381,40 @@
     ]
     o_wide[...] = o_all[...].astype(F32)
     stat = sum(o_wide[pl.ds(STAT + i, HEADS, stride=SLOT), :] for i in range(3))
-    for s in range(STEPS):
-        for r in range(REQ):
-            i = s * REQ + r
-            mass_o[s, r] = (lse_all[slot(i)] - stat[:, LOW + i : LOW + i + 1])[:, :n_local]
+    stat = jnp.concatenate([stat, jnp.zeros((HD - HEADS, HD), F32)], axis=0).T
+    for r in range(REQ):
+        blocks = lse_all[r // 2]
+        for s in range(STEPS):
+            i = LOW + s * REQ + r
+            at_lane = (r % 2) * (HD // 2) + s * HEADS
+            moved = pltpu.roll(blocks, HD - at_lane, 1) if at_lane else blocks
+            mass_v[s, :, r, :] = (moved - stat[i : i + 1])[:n_local, :HEADS]
+    mass_out = pltpu.make_async_copy(mass_v, mass_o, out_sem.at[0])
+    mass_out.start()
     for one in got:
         one.wait_recv()
     term = term.astype(F32)
     for k in range(1, 4):
         term = term + x_in[slot(k - 1), :cols].astype(F32)
     for s in range(STEPS):
-        out_o[s] = term[s * REQ : (s + 1) * REQ].astype(BF16)
+        out_v[s] = term[s * REQ : (s + 1) * REQ].astype(BF16)
+    layer_out = pltpu.make_async_copy(out_v, out_o, out_sem.at[1])
+    layer_out.start()
     for one in sends:
         one.wait_send()
+    mass_out.wait()
+    layer_out.wait()
+
+
+def hand_on(mass_i, out_i, mass_o, out_o, sem):
+    copies = [
+        pltpu.make_async_copy(mass_i, mass_o, sem.at[0]),
+        pltpu.make_async_copy(out_i, out_o, sem.at[1]),
+    ]
+    for one in copies:
+        one.start()
+    for one in copies:
+        one.wait()
 
 
 def body(hidden, w_query, q_gain, basis, keys, values, new_keys, new_values, block_lists, w_out):
@@ -378,14 +433,15 @@
         refs[5] = refs[5].at[:, 0]
         kernel(*refs)
 
-    return pl.pallas_call(
+    shapes = (
+        jax.ShapeDtypeStruct((STEPS, n_local, REQ, HEADS), F32),
+        jax.ShapeDtypeStruct((STEPS, REQ, w_out.shape[1]), BF16),
+    )
+    raw = pl.pallas_call(
         run,
-        out_shape=(
-            jax.ShapeDtypeStruct((STEPS, REQ, HEADS, n_local), F32),
-            jax.ShapeDtypeStruct((STEPS, REQ, w_out.shape[1]), BF16),
-        ),
-        in_specs=[pl.BlockSpec(memory_space=pltpu.HBM)] * len(ops),
-        out_specs=(pl.BlockSpec(memory_space=pltpu.VMEM),) * 2,
+        out_shape=shapes,
+        in_specs=[pl.BlockSpec(memory_space=pl.ANY)] * len(ops),
+        out_specs=(pl.BlockSpec(memory_space=pl.ANY),) * 2,
         scratch_shapes=landing
         + [
             pltpu.VMEM((SLOT, block_lists.shape[3]), jnp.int32),
@@ -394,15 +450,30 @@
             slots(STEPS),
             pltpu.VMEM((6 * HD, HD), BF16),
             pltpu.VMEM((w_out.shape[0], w_out.shape[1]), BF16),
+            pltpu.VMEM((REQ, HD, n_tok), BF16),
+            pltpu.VMEM((REQ // 2, n_tok, 2 * HD), BF16),
+            pltpu.VMEM(shapes[0].shape, F32),
+            pltpu.VMEM(shapes[1].shape, BF16),
         ]
-        + [slots(n) for n in (16, 15, 1, 7, 16, 16, 12)]
+        + [slots(n) for n in (16, 15, 1, 7, 16, 16)]
+        + [pltpu.VMEM((REQ // 2, SLOT, HD), F32)]
         + [slots(n, BF16) for n in (16, 15, 1, 7, 16, 1, 3)]
-        + [dma(n) for n in (10, 30, 30, 14, 14, 30, 30, 3, 3)],
+        + [dma(n) for n in (10, 2, 30, 30, 14, 14, 30, 30, 3, 3)],
         compiler_params=pltpu.CompilerParams(
             collective_id=0, has_side_effects=True, vmem_limit_bytes=60 * 2**20
         ),
         name="decode",
     )(*ops)
+    mass, layer_out = pl.pallas_call(
+        hand_on,
+        out_shape=shapes,
+        in_specs=[pl.BlockSpec(memory_space=pl.ANY)] * 2,
+        out_specs=(pl.BlockSpec(memory_space=pl.ANY),) * 2,
+        scratch_shapes=[dma(2)],
+        compiler_params=pltpu.CompilerParams(vmem_limit_bytes=60 * 2**20),
+        name="hand_on",
+    )(*raw)
+    return mass.transpose(0, 2, 3, 1), layer_out
 
 
 def solution(mesh):

time: 56.8 us -> 55.2 us (0.972)
  local copies, waits for them, and re-layouts: 2.93 us -> 0 us
  Pallas kernels: 53 us -> 54.4 us
    pallas_call x1 -> x0, local copies, waits for them, and re-layouts: 1.67 us -> none  [body(): pl.pallas_call(run, out_shape=(jax.ShapeDtypeStruct((STEPS, REQ, HEADS, n...]
    pallas_call x1 -> x2, Pallas kernels: 53 us -> 54.4 us  [the longest x1 51 us: body(): pl.pallas_call(run, out_shape=shapes, in_specs=[pl.BlockSpec(memory_space...]
    unnamed x1 -> x0, local copies, waits for them, and re-layouts: 1.26 us -> none
where the time goes in v3:
time: 55.2 us; the launch traced here: 55.1 us
  Pallas kernels  54.4 us (99%)
  between operations  0.64 us (1%)
    pallas_call x1, Pallas kernels, body(): pl.pallas_call(run, out_shape=shapes, in_specs=[pl.BlockSpec(memory_space...  51 us
    pallas_call x1, Pallas kernels, body(): pl.pallas_call(hand_on, out_shape=shapes, in_specs=[pl.BlockSpec(memory_s...  3.45 us

profile of v3, /device:TPU:1, one launch (start us, length us, event | category | flops | bytes accessed | tf_op | source)
XLA Modules:
  0.0 55.1 jit_solution(15515083023100727089)
XLA Ops:
  0.6 51.0 %decode.1 = (f32[3,12,4,16]{3,2,1,0:T(4,128)}, bf16[3,4,32]{2,1,0:T(4,128)(2,1)}) custom-call(bf16[3,4,32]{2,1,0:T(4,128)(2,1)} %refs_0_.1, bf16[32,2048]{1,0:T(8,128)(2,1)} %refs_1_.1, f32[128]{0:T(128)} %refs_2_.1, f32[1,128,128]{2,1,0:T(8,128)} %refs_3_.1, bf16[4,1,1536,128]{3,2,1,0:T(8,128)(2,1)} %refs_4_.1, bf16[4,1,1536,128]{3,2,1,0:T(8,128)(2,1)} %refs_5_.1, ...), custom_call_target="tpu_custom_call" | custom-call | tf_op jit(solution)/shard_map/decode/pallas_call | solution.py:440
  51.6 3.4 %hand_on.1 = (f32[3,12,4,16]{3,2,1,0:T(4,128)}, bf16[3,4,32]{2,1,0:T(4,128)(2,1)}) custom-call(f32[3,12,4,16]{3,2,1,0:T(4,128)} %get-tuple-element.6.mass_i, bf16[3,4,32]{2,1,0:T(4,128)(2,1)} %get-tuple-element.7.out_i), custom_call_target="tpu_custom_call" | custom-call | tf_op jit(solution)/shard_map/hand_on/pallas_call | solution.py:467

commit v4 on v3

--- a/solution.py
+++ b/solution.py
@@ -78,11 +78,11 @@
     hid_h, wq_h, gain_h, basis_h, keys_h, vals_h, nk_h, nv_h, lists_h, wo_h,
     mass_o, out_o,
     hid_v, wq_v, gain_v, basis_v, keys_v, vals_v, nk_v, nv_v, lists_v, wo_v,
-    list_rows, bias, nk_rows, nv_rows, rot, wo_t, keys_t, low_keys, mass_v, out_v,
+    list_rows, bias, nk_rows, nv_rows, rot, wo_t, keys_t, low_keys,
     q_part, q_rs, q_own, q_ex, q_all,
     o_wide, lse_all,
     o_part, o_rs, o_own, o_ex, o_all, x_own, x_in,
-    in_sem, out_sem, rs_s, rs_r, ex_s, ex_r, ag_s, ag_r, x_s, x_r,
+    in_sem, rs_s, rs_r, ex_s, ex_r, ag_s, ag_r, x_s, x_r,
 ):
     ctx = lax.axis_index("ctx")
     x = lax.axis_index("kvh")
@@ -388,22 +388,16 @@
             i = LOW + s * REQ + r
             at_lane = (r % 2) * (HD // 2) + s * HEADS
             moved = pltpu.roll(blocks, HD - at_lane, 1) if at_lane else blocks
-            mass_v[s, :, r, :] = (moved - stat[i : i + 1])[:n_local, :HEADS]
-    mass_out = pltpu.make_async_copy(mass_v, mass_o, out_sem.at[0])
-    mass_out.start()
+            mass_o[s, :, r, :] = (moved - stat[i : i + 1])[:n_local, :HEADS]
     for one in got:
         one.wait_recv()
     term = term.astype(F32)
     for k in range(1, 4):
         term = term + x_in[slot(k - 1), :cols].astype(F32)
     for s in range(STEPS):
-        out_v[s] = term[s * REQ : (s + 1) * REQ].astype(BF16)
-    layer_out = pltpu.make_async_copy(out_v, out_o, out_sem.at[1])
-    layer_out.start()
+        out_o[s] = term[s * REQ : (s + 1) * REQ].astype(BF16)
     for one in sends:
         one.wait_send()
-    mass_out.wait()
-    layer_out.wait()
 
 
 def hand_on(mass_i, out_i, mass_o, out_o, sem):
@@ -422,6 +416,7 @@
     n_local = n_tok // BLK
     new_keys, new_values = new_keys[:, :, 0], new_values[:, :, 0]
     ops = (hidden, w_query, q_gain, basis, keys, values, new_keys, new_values, block_lists, w_out.T)
+    ops = tuple(pltpu.with_memory_space_constraint(o, pltpu.HBM) for o in ops)
     slots = lambda n, kind=F32: pltpu.VMEM((n * SLOT, HD), kind)
     landing = [pltpu.VMEM(o.shape, o.dtype) for o in ops]
     landing[4] = landing[5] = pltpu.VMEM((REQ, n_tok, HD), BF16)
@@ -441,7 +436,7 @@
         run,
         out_shape=shapes,
         in_specs=[pl.BlockSpec(memory_space=pl.ANY)] * len(ops),
-        out_specs=(pl.BlockSpec(memory_space=pl.ANY),) * 2,
+        out_specs=(pl.BlockSpec(memory_space=pltpu.VMEM),) * 2,
         scratch_shapes=landing
         + [
             pltpu.VMEM((SLOT, block_lists.shape[3]), jnp.int32),
@@ -452,15 +447,13 @@
             pltpu.VMEM((w_out.shape[0], w_out.shape[1]), BF16),
             pltpu.VMEM((REQ, HD, n_tok), BF16),
             pltpu.VMEM((REQ // 2, n_tok, 2 * HD), BF16),
-            pltpu.VMEM(shapes[0].shape, F32),
-            pltpu.VMEM(shapes[1].shape, BF16),
         ]
         + [slots(n) for n in (16, 15, 1, 7, 16, 16)]
         + [pltpu.VMEM((REQ // 2, SLOT, HD), F32)]
         + [slots(n, BF16) for n in (16, 15, 1, 7, 16, 1, 3)]
-        + [dma(n) for n in (10, 2, 30, 30, 14, 14, 30, 30, 3, 3)],
+        + [dma(n) for n in (10, 30, 30, 14, 14, 30, 30, 3, 3)],
         compiler_params=pltpu.CompilerParams(
-            collective_id=0, has_side_effects=True, vmem_limit_bytes=60 * 2**20
+            collective_id=0, has_side_effects=True, vmem_limit_bytes=32 * 2**20
         ),
         name="decode",
     )(*ops)
@@ -470,7 +463,7 @@
         in_specs=[pl.BlockSpec(memory_space=pl.ANY)] * 2,
         out_specs=(pl.BlockSpec(memory_space=pl.ANY),) * 2,
         scratch_shapes=[dma(2)],
-        compiler_params=pltpu.CompilerParams(vmem_limit_bytes=60 * 2**20),
+        compiler_params=pltpu.CompilerParams(vmem_limit_bytes=32 * 2**20),
         name="hand_on",
     )(*raw)
     return mass.transpose(0, 2, 3, 1), layer_out

time: 55.2 us -> 51.9 us (0.940)
  Pallas kernels: 54.4 us -> 51.1 us
    pallas_call x1, Pallas kernels: 3.45 us -> 0.65 us  [body(): pl.pallas_call(hand_on, out_shape=shapes, in_specs=[pl.BlockSpec(memory_s...]
where the time goes in v4:
time: 51.9 us; the launch traced here: 51.8 us
  Pallas kernels  51.1 us (98%)
  between operations  0.64 us (1%)
    pallas_call x1, Pallas kernels, body(): pl.pallas_call(run, out_shape=shapes, in_specs=[pl.BlockSpec(memory_space...  50.5 us

profile of v4, /device:TPU:1, one launch (start us, length us, event | category | flops | bytes accessed | tf_op | source)
XLA Modules:
  0.0 51.8 jit_solution(15477663130054764889)
XLA Ops:
  0.6 50.5 %decode.1 = (f32[3,12,4,16]{3,2,1,0:T(4,128)S(1)}, bf16[3,4,32]{2,1,0:T(4,128)(2,1)S(1)}) custom-call(bf16[3,4,32]{2,1,0:T(4,128)(2,1)} %refs_0_.1, bf16[32,2048]{1,0:T(8,128)(2,1)} %refs_1_.1, f32[128]{0:T(128)} %refs_2_.1, f32[1,128,128]{2,1,0:T(8,128)} %refs_3_.1, bf16[4,1,1536,128]{3,2,1,0:T(8,128)(2,1)} %refs_4_.1, bf16[4,1,1536,128]{3,2,1,0:T(8,128)(2,1)} %refs_5_.1, ...), custom_call_target="tpu_custom_call" | custom-call | tf_op jit(solution)/shard_map/decode/pallas_call | solution.py:435
  51.1 0.7 %hand_on.1 = (f32[3,12,4,16]{3,2,1,0:T(4,128)}, bf16[3,4,32]{2,1,0:T(4,128)(2,1)}) custom-call(f32[3,12,4,16]{3,2,1,0:T(4,128)S(1)} %get-tuple-element.6.mass_i, bf16[3,4,32]{2,1,0:T(4,128)(2,1)S(1)} %get-tuple-element.7.out_i), custom_call_target="tpu_custom_call" | custom-call | tf_op jit(solution)/shard_map/hand_on/pallas_call | solution.py:460

commit v5 on v4

--- a/solution.py
+++ b/solution.py
@@ -12,12 +12,15 @@
 ROWS = STEPS * REQ
 SLOT = 16
 STAT = 12
-LOW = 16
 HEADS = 16
 HALF = 8
 HD = 128
 NONE = -1e30
 FAR_FIRST = (4, 3, 5, 2, 6, 1, 7)
+NEAR = (7, 0, 6, 8, 14, 1, 5, 9, 13)
+FAR = (2, 4, 10, 12, 3, 11)
+NEAR_RING = (0, 6, 1, 5)
+FAR_RING = (2, 4, 3)
 MESH = pl.DeviceIdType.MESH
 F32 = jnp.float32
 BF16 = jnp.bfloat16
@@ -81,8 +84,8 @@
     list_rows, bias, nk_rows, nv_rows, rot, wo_t, keys_t, low_keys,
     q_part, q_rs, q_own, q_ex, q_all,
     o_wide, lse_all,
-    o_part, o_rs, o_own, o_ex, o_all, x_own, x_in,
-    in_sem, rs_s, rs_r, ex_s, ex_r, ag_s, ag_r, x_s, x_r,
+    o_part, o_rs, o_own, o_ex, o_all, x_own, x_in, low_own, low_in,
+    in_sem, rs_s, rs_r, ex_s, ex_r, ag_s, ag_r, x_s, x_r, low_s, low_r,
 ):
     ctx = lax.axis_index("ctx")
     x = lax.axis_index("kvh")
@@ -123,7 +126,7 @@
     barrier = pltpu.get_barrier_semaphore()
     partners = []
     for k in FAR_FIRST:
-        partners += [dev_a(k), dev_b(k), cross_a(k), cross_b(k)]
+        partners += [dev_a(k), dev_b(k), cross_a(k)]
     partners += [dev_x(2), dev_x(1), dev_x(3), cross_a(0)]
     for who in partners:
         pl.semaphore_signal(barrier, inc=1, device_id=who, device_id_type=MESH)
@@ -162,17 +165,17 @@
 
     def gather(buf, cut, base):
         got = {}
+        for k in FAR_FIRST:
+            got[k - 1] = send(
+                buf.at[cut(mine)], buf.at[cut(mine)],
+                ag_s.at[base + k - 1], ag_r.at[base + k - 1], dev_a(k),
+            )
         for k in FAR_FIRST + (0,):
-            if k:
-                got[k - 1] = send(
-                    buf.at[cut(mine)], buf.at[cut(mine)],
-                    ag_s.at[base + k - 1], ag_r.at[base + k - 1], dev_a(k),
-                )
             got[7 + k] = send(
                 buf.at[cut(mine)], buf.at[cut(mine)],
                 ag_s.at[base + 7 + k], ag_r.at[base + 7 + k], cross_a(k),
             )
-        return [got[i] for i in range(15)]
+        return [got[i] for i in NEAR + FAR]
 
     def exchange(own, into, cut, base):
         got = {}
@@ -182,6 +185,22 @@
                 ex_s.at[base + k - 1], ex_r.at[base + k - 1], dev_b(k),
             )
         return [got[i] for i in range(7)]
+
+    def low_ring(stage, dev):
+        got = {}
+        for k in FAR_FIRST:
+            i = 7 * stage + k - 1
+            got[k - 1] = send(low_own.at[stage], low_in.at[i], low_s.at[i], low_r.at[i], dev(k))
+        return [got[i] for i in range(7)]
+
+    def low_join(stage, got):
+        for one in got:
+            one.wait_recv()
+        parts = [low_own[stage]] + [low_in[7 * stage + i] for i in range(len(got))]
+        top = parts[0]
+        for one in parts[1:]:
+            top = jnp.maximum(top, one)
+        low_own[stage + 1] = top + jnp.log(sum(jnp.exp(one - top) for one in parts))
 
     fetch[0].wait()
     fetch[1].wait()
@@ -230,7 +249,7 @@
         keys_t[r] = keys_v[r].T
 
     total = q_part[slot(mine)]
-    for k in range(15):
+    for k in NEAR + FAR:
         got[k].wait_recv()
         total = total + q_rs[slot(k)]
     total = jnp.where(iota((SLOT, HD), 0) < ROWS, total, 0.0)
@@ -241,7 +260,7 @@
         low_keys[r // 2, :, (r % 2) * HD : (r % 2 + 1) * HD] = jnp.dot(
             keys_v[r], copies, preferred_element_type=F32
         ).astype(BF16)
-    for k in range(7):
+    for k in NEAR_RING + FAR_RING:
         got[k].wait_recv()
         total = total + q_ex[slot(k)]
     total = jnp.where(iota((SLOT, HD), 0) < ROWS, total, 0.0)
@@ -293,6 +312,12 @@
             rows = slice(s * HEADS, (s + 1) * HEADS)
             o_wide[pl.ds(i, HEADS, stride=SLOT), :] = acc[rows]
             stat = jnp.where(lane16 == i, lse[rows], stat)
+    for i, piece in enumerate(split3(stat)):
+        o_wide[pl.ds(STAT + i, HEADS, stride=SLOT), :] = piece.astype(F32)
+    o_wide[pl.ds(SLOT - 1, HEADS, stride=SLOT), :] = jnp.zeros((HEADS, HD), F32)
+    o_part[...] = o_wide[...].astype(BF16)
+
+    got = scatter(o_part, o_rs, slot, 15)
     lane48 = iota((n_rows, HD), 1)
     for pair in range(REQ // 2):
         sides = []
@@ -319,24 +344,12 @@
             peak = jnp.max(part, axis=0, keepdims=True)
             rows.append(peak + jnp.log(jnp.sum(jnp.exp(part - peak), axis=0, keepdims=True)))
         blocks = jnp.concatenate(rows, axis=0)
+        lse_all[pair, :n_local] = blocks
         peak = jnp.max(blocks, axis=0, keepdims=True)
-        low_lse = peak + jnp.log(jnp.sum(jnp.exp(blocks - peak), axis=0, keepdims=True))
-        lse_all[pair, :n_local] = blocks
-        low_lse = jnp.broadcast_to(low_lse, (8, HD)).T
-        for half in range(2):
-            for s in range(STEPS):
-                at_row = half * (HD // 2) + s * HEADS
-                stat = jnp.where(
-                    lane16 == LOW + s * REQ + 2 * pair + half,
-                    low_lse[at_row : at_row + HEADS, :1],
-                    stat,
-                )
-    for i, piece in enumerate(split3(stat)):
-        o_wide[pl.ds(STAT + i, HEADS, stride=SLOT), :] = piece.astype(F32)
-    o_wide[pl.ds(SLOT - 1, HEADS, stride=SLOT), :] = jnp.zeros((HEADS, HD), F32)
-    o_part[...] = o_wide[...].astype(BF16)
-
-    got = scatter(o_part, o_rs, slot, 15)
+        low_own[0, pair : pair + 1] = peak + jnp.log(
+            jnp.sum(jnp.exp(blocks - peak), axis=0, keepdims=True)
+        )
+    low_got = low_ring(0, dev_a)
     row16 = iota((SLOT, 1), 0)
     fresh = [
         jnp.where(
@@ -356,18 +369,34 @@
     new_row = jnp.sum(jnp.where(diag, top + jnp.log(new_sum), 0.0), axis=0, keepdims=True)
     new_row = jnp.where(iota((1, HD), 1) < ROWS, new_row, NONE)
 
-    for one in got:
-        one.wait_recv()
-    outs = [o_wide[slot(mine)]] + [o_rs[slot(k)].astype(F32) for k in range(15)]
+    outs = [o_wide[slot(mine)]]
+    for k in NEAR:
+        got[k].wait_recv()
+        outs.append(o_rs[slot(k)].astype(F32))
     res, row = merge(outs, [stat_of(p) for p in outs])
+    outs = []
+    for k in FAR:
+        got[k].wait_recv()
+        outs.append(o_rs[slot(k)].astype(F32))
+    res, row = merge([res] + outs, [row] + [stat_of(p) for p in outs])
     o_own[...] = with_stat(res, row)
     got = exchange(o_own, o_ex, slot, 7)
-    for one in got:
-        one.wait_recv()
-    outs = [o_ex[slot(k)].astype(F32) for k in range(7)]
+    low_join(0, low_got)
+    low_got = low_ring(1, dev_b)
+    outs = []
+    for k in NEAR_RING:
+        got[k].wait_recv()
+        outs.append(o_ex[slot(k)].astype(F32))
     res, row = merge([res, new_o] + outs, [row, new_row] + [stat_of(p) for p in outs])
-    o_all[slot(mine)] = with_stat(res, row)
+    outs = []
+    for k in FAR_RING:
+        got[k].wait_recv()
+        outs.append(o_ex[slot(k)].astype(F32))
+    res, row = merge([res] + outs, [row] + [stat_of(p) for p in outs])
+    o_all[slot(mine)] = jnp.where(iota((SLOT, HD), 0) < ROWS, res, 0.0).astype(BF16)
     got = gather(o_all, slot, 15)
+    low_join(1, low_got)
+    low_last = send(low_own.at[2], low_in.at[14], low_s.at[14], low_r.at[14], cross_a(0))
     for one in got:
         one.wait_recv()
 
@@ -378,17 +407,15 @@
     got = [
         send(x_own, x_in.at[slot(k - 1)], x_s.at[k - 1], x_r.at[k - 1], dev_x(k))
         for k in (2, 1, 3)
-    ]
-    o_wide[...] = o_all[...].astype(F32)
-    stat = sum(o_wide[pl.ds(STAT + i, HEADS, stride=SLOT), :] for i in range(3))
-    stat = jnp.concatenate([stat, jnp.zeros((HD - HEADS, HD), F32)], axis=0).T
+    ][::-1]
+    low_join(2, [low_last])
     for r in range(REQ):
-        blocks = lse_all[r // 2]
+        pair = r // 2
+        mass = lse_all[pair] - low_own[3, pair : pair + 1]
         for s in range(STEPS):
-            i = LOW + s * REQ + r
             at_lane = (r % 2) * (HD // 2) + s * HEADS
-            moved = pltpu.roll(blocks, HD - at_lane, 1) if at_lane else blocks
-            mass_o[s, :, r, :] = (moved - stat[i : i + 1])[:n_local, :HEADS]
+            moved = pltpu.roll(mass, HD - at_lane, 1) if at_lane else mass
+            mass_o[s, :, r, :] = moved[:n_local, :HEADS]
     for one in got:
         one.wait_recv()
     term = term.astype(F32)
@@ -451,7 +478,8 @@
         + [slots(n) for n in (16, 15, 1, 7, 16, 16)]
         + [pltpu.VMEM((REQ // 2, SLOT, HD), F32)]
         + [slots(n, BF16) for n in (16, 15, 1, 7, 16, 1, 3)]
-        + [dma(n) for n in (10, 30, 30, 14, 14, 30, 30, 3, 3)],
+        + [pltpu.VMEM((n, REQ // 2, HD), F32) for n in (4, 15)]
+        + [dma(n) for n in (10, 30, 30, 14, 14, 30, 30, 3, 3, 15, 15)],
         compiler_params=pltpu.CompilerParams(
             collective_id=0, has_side_effects=True, vmem_limit_bytes=32 * 2**20
         ),

time: 51.9 us -> 51.1 us (0.985)
  Pallas kernels: 51.1 us -> 50.3 us
    pallas_call x1, Pallas kernels: 50.5 us -> 49.7 us  [body(): pl.pallas_call(run, out_shape=shapes, in_specs=[pl.BlockSpec(memory_space...]
where the time goes in v5:
time: 51.1 us; the launch traced here: 51 us
  Pallas kernels  50.3 us (98%)
  between operations  0.64 us (1%)
    pallas_call x1, Pallas kernels, body(): pl.pallas_call(run, out_shape=shapes, in_specs=[pl.BlockSpec(memory_space...  49.7 us

profile of v5, /device:TPU:1, one launch (start us, length us, event | category | flops | bytes accessed | tf_op | source)
XLA Modules:
  0.0 51.0 jit_solution(9844587303716876851)
XLA Ops:
  0.6 49.7 %decode.1 = (f32[3,12,4,16]{3,2,1,0:T(4,128)S(1)}, bf16[3,4,32]{2,1,0:T(4,128)(2,1)S(1)}) custom-call(bf16[3,4,32]{2,1,0:T(4,128)(2,1)} %refs_0_.1, bf16[32,2048]{1,0:T(8,128)(2,1)} %refs_1_.1, f32[128]{0:T(128)} %refs_2_.1, f32[1,128,128]{2,1,0:T(8,128)} %refs_3_.1, bf16[4,1,1536,128]{3,2,1,0:T(8,128)(2,1)} %refs_4_.1, bf16[4,1,1536,128]{3,2,1,0:T(8,128)(2,1)} %refs_5_.1, ...), custom_call_target="tpu_custom_call" | custom-call | tf_op jit(solution)/shard_map/decode/pallas_call | solution.py:462
  50.3 0.7 %hand_on.1 = (f32[3,12,4,16]{3,2,1,0:T(4,128)}, bf16[3,4,32]{2,1,0:T(4,128)(2,1)}) custom-call(f32[3,12,4,16]{3,2,1,0:T(4,128)S(1)} %get-tuple-element.6.mass_i, bf16[3,4,32]{2,1,0:T(4,128)(2,1)S(1)} %get-tuple-element.7.out_i), custom_call_target="tpu_custom_call" | custom-call | tf_op jit(solution)/shard_map/hand_on/pallas_call | solution.py:488

commit v6 on v5

--- a/solution.py
+++ b/solution.py
@@ -85,7 +85,7 @@
     q_part, q_rs, q_own, q_ex, q_all,
     o_wide, lse_all,
     o_part, o_rs, o_own, o_ex, o_all, x_own, x_in, low_own, low_in,
-    in_sem, rs_s, rs_r, ex_s, ex_r, ag_s, ag_r, x_s, x_r, low_s, low_r,
+    in_sem, s_sem, r_sem,
 ):
     ctx = lax.axis_index("ctx")
     x = lax.axis_index("kvh")
@@ -138,65 +138,49 @@
     for one in fetch:
         one.start()
 
-    sends = []
 
     def send(src, dst, s_sem, r_sem, who):
-        copy = pltpu.make_async_remote_copy(
+        pltpu.make_async_remote_copy(
             src_ref=src, dst_ref=dst, send_sem=s_sem, recv_sem=r_sem,
             device_id=who, device_id_type=MESH,
-        )
-        copy.start()
-        sends.append(copy)
-        return copy
-
-    def scatter(part, into, cut, base):
-        got = {}
+        ).start()
+
+    def scatter(part, into, cut, s_sem, r_sem):
         for k in FAR_FIRST + (0,):
             if k:
-                got[k - 1] = send(
+                send(
                     part.at[cut(c * HALF + ring_a(k))], into.at[cut(k - 1)],
-                    rs_s.at[base + k - 1], rs_r.at[base + k - 1], dev_a(k),
+                    s_sem, r_sem[k - 1 in FAR], dev_a(k),
                 )
-            got[7 + k] = send(
+            send(
                 part.at[cut(theirs + ring_b(k))], into.at[cut(7 + k)],
-                rs_s.at[base + 7 + k], rs_r.at[base + 7 + k], cross_b(k),
+                s_sem, r_sem[7 + k in FAR], cross_b(k),
             )
-        return [got[i] for i in range(15)]
-
-    def gather(buf, cut, base):
-        got = {}
+
+    def gather(buf, cut, s_sem, r_sem):
         for k in FAR_FIRST:
-            got[k - 1] = send(
-                buf.at[cut(mine)], buf.at[cut(mine)],
-                ag_s.at[base + k - 1], ag_r.at[base + k - 1], dev_a(k),
+            send(buf.at[cut(mine)], buf.at[cut(mine)], s_sem, r_sem, dev_a(k))
+        for k in FAR_FIRST + (0,):
+            send(buf.at[cut(mine)], buf.at[cut(mine)], s_sem, r_sem, cross_a(k))
+
+    def exchange(own, into, cut, s_sem, r_sem):
+        for k in FAR_FIRST:
+            send(
+                own.at[cut(0)], into.at[cut(k - 1)],
+                s_sem, r_sem[k - 1 in FAR_RING], dev_b(k),
             )
-        for k in FAR_FIRST + (0,):
-            got[7 + k] = send(
-                buf.at[cut(mine)], buf.at[cut(mine)],
-                ag_s.at[base + 7 + k], ag_r.at[base + 7 + k], cross_a(k),
-            )
-        return [got[i] for i in NEAR + FAR]
-
-    def exchange(own, into, cut, base):
-        got = {}
+
+    def take(ref, rows, sem):
+        some = ref.at[pl.ds(0, rows)]
+        pltpu.make_async_copy(some, some, sem).wait()
+
+    def low_ring(stage, dev):
         for k in FAR_FIRST:
-            got[k - 1] = send(
-                own.at[cut(0)], into.at[cut(k - 1)],
-                ex_s.at[base + k - 1], ex_r.at[base + k - 1], dev_b(k),
-            )
-        return [got[i] for i in range(7)]
-
-    def low_ring(stage, dev):
-        got = {}
-        for k in FAR_FIRST:
-            i = 7 * stage + k - 1
-            got[k - 1] = send(low_own.at[stage], low_in.at[i], low_s.at[i], low_r.at[i], dev(k))
-        return [got[i] for i in range(7)]
-
-    def low_join(stage, got):
-        for one in got:
-            one.wait_recv()
-        parts = [low_own[stage]] + [low_in[7 * stage + i] for i in range(len(got))]
+            send(low_own.at[stage], low_in.at[7 * stage + k - 1], s_sem.at[7], r_sem.at[11 + stage], dev(k))
+
+    def low_join(stage, count):
+        take(low_in, count, r_sem.at[11 + stage])
+        parts = [low_own[stage]] + [low_in[7 * stage + i] for i in range(count)]
         top = parts[0]
         for one in parts[1:]:
             top = jnp.maximum(top, one)
@@ -214,10 +198,46 @@
         )
     pl.semaphore_wait(barrier, len(partners))
 
-    got = scatter(q_part, q_rs, rows_of, 0)
-    for one in fetch[2:9]:
-        one.wait()
-
+    scatter(q_part, q_rs, rows_of, s_sem.at[0], (r_sem.at[0], r_sem.at[1]))
+    for i in (2, 3, 8):
+        fetch[i].wait()
+
+    b_hi, b_mid, b_lo = split3(basis_v[0])
+    for i, piece in enumerate((b_hi, b_mid, b_lo, b_hi, b_mid, b_hi)):
+        rot[i * HD : (i + 1) * HD, :] = piece
+    gain = gain_v[...].reshape(1, HD)
+
+    for r in range(REQ // 2):
+        keys_t[r] = keys_v[r].T
+
+    total = q_part[slot(mine)]
+    for group, sem in ((NEAR, r_sem.at[0]), (FAR, r_sem.at[1])):
+        take(q_rs, len(group) * ROWS, sem)
+        total = total + sum(q_rs[slot(k)] for k in group)
+    total = jnp.where(iota((SLOT, HD), 0) < ROWS, total, 0.0)
+    q_own[...] = total
+    exchange(q_own, q_ex, rows_of, s_sem.at[1], (r_sem.at[2], r_sem.at[3]))
+    for r in range(REQ // 2, REQ):
+        keys_t[r] = keys_v[r].T
+
+    for group, sem in ((NEAR_RING, r_sem.at[2]), (FAR_RING, r_sem.at[3])):
+        take(q_ex, len(group) * ROWS, sem)
+        total = total + sum(q_ex[slot(k)] for k in group)
+    total = jnp.where(iota((SLOT, HD), 0) < ROWS, total, 0.0)
+
+    scale = HD ** (-0.5)
+    norm = lax.rsqrt(jnp.mean(total * total, axis=1, keepdims=True) + 1e-06) * scale
+    g_hi, g_mid, g_lo = split3(total * gain)
+    turned = jnp.dot(
+        jnp.concatenate([g_hi, g_hi, g_hi, g_mid, g_mid, g_lo], axis=1),
+        rot[...],
+        preferred_element_type=F32,
+    )
+    q_mine = turned * norm
+    q_all[slot(mine)] = q_mine
+    gather(q_all, rows_of, s_sem.at[2], r_sem.at[4])
+    for i in (4, 5, 6, 7, 9):
+        fetch[i].wait()
     list_rows[...] = jnp.full(list_rows.shape, -1, jnp.int32)
     for s in range(STEPS):
         for r in range(REQ):
@@ -240,45 +260,13 @@
         bias[:, blk * BLK : (blk + 1) * BLK] = jnp.broadcast_to(
             jnp.where(hit > 0.5, 0.0, NONE), (SLOT, BLK)
         )
-    b_hi, b_mid, b_lo = split3(basis_v[0])
-    for i, piece in enumerate((b_hi, b_mid, b_lo, b_hi, b_mid, b_hi)):
-        rot[i * HD : (i + 1) * HD, :] = piece
-    gain = gain_v[...].reshape(1, HD)
-    wo_t[...] = wo_v[...].astype(F32).T.astype(BF16)
-    for r in range(REQ):
-        keys_t[r] = keys_v[r].T
-
-    total = q_part[slot(mine)]
-    for k in NEAR + FAR:
-        got[k].wait_recv()
-        total = total + q_rs[slot(k)]
-    total = jnp.where(iota((SLOT, HD), 0) < ROWS, total, 0.0)
-    q_own[...] = total
-    got = exchange(q_own, q_ex, rows_of, 0)
     copies = (iota((HD, HD), 0) == lax.rem(iota((HD, HD), 1), RANK)).astype(F32).astype(BF16)
     for r in range(REQ):
         low_keys[r // 2, :, (r % 2) * HD : (r % 2 + 1) * HD] = jnp.dot(
             keys_v[r], copies, preferred_element_type=F32
         ).astype(BF16)
-    for k in NEAR_RING + FAR_RING:
-        got[k].wait_recv()
-        total = total + q_ex[slot(k)]
-    total = jnp.where(iota((SLOT, HD), 0) < ROWS, total, 0.0)
-
-    scale = HD ** (-0.5)
-    norm = lax.rsqrt(jnp.mean(total * total, axis=1, keepdims=True) + 1e-06) * scale
-    g_hi, g_mid, g_lo = split3(total * gain)
-    turned = jnp.dot(
-        jnp.concatenate([g_hi, g_hi, g_hi, g_mid, g_mid, g_lo], axis=1),
-        rot[...],
-        preferred_element_type=F32,
-    )
-    q_mine = turned * norm
-    q_all[slot(mine)] = q_mine
-    got = gather(q_all, rows_of, 0)
-    fetch[9].wait()
-    for one in got:
-        one.wait_recv()
+
+    take(q_all, 15 * ROWS, r_sem.at[4])
 
     lane16 = iota((HEADS, HD), 1)
     stat = jnp.zeros((HEADS, HD), F32)
@@ -317,7 +305,7 @@
     o_wide[pl.ds(SLOT - 1, HEADS, stride=SLOT), :] = jnp.zeros((HEADS, HD), F32)
     o_part[...] = o_wide[...].astype(BF16)
 
-    got = scatter(o_part, o_rs, slot, 15)
+    scatter(o_part, o_rs, slot, s_sem.at[3], (r_sem.at[5], r_sem.at[6]))
     lane48 = iota((n_rows, HD), 1)
     for pair in range(REQ // 2):
         sides = []
@@ -349,7 +337,7 @@
         low_own[0, pair : pair + 1] = peak + jnp.log(
             jnp.sum(jnp.exp(blocks - peak), axis=0, keepdims=True)
         )
-    low_got = low_ring(0, dev_a)
+    low_ring(0, dev_a)
     row16 = iota((SLOT, 1), 0)
     fresh = [
         jnp.where(
@@ -370,45 +358,43 @@
     new_row = jnp.where(iota((1, HD), 1) < ROWS, new_row, NONE)
 
     outs = [o_wide[slot(mine)]]
+    take(o_rs, len(NEAR) * SLOT, r_sem.at[5])
     for k in NEAR:
-        got[k].wait_recv()
         outs.append(o_rs[slot(k)].astype(F32))
     res, row = merge(outs, [stat_of(p) for p in outs])
     outs = []
+    take(o_rs, len(FAR) * SLOT, r_sem.at[6])
     for k in FAR:
-        got[k].wait_recv()
         outs.append(o_rs[slot(k)].astype(F32))
     res, row = merge([res] + outs, [row] + [stat_of(p) for p in outs])
     o_own[...] = with_stat(res, row)
-    got = exchange(o_own, o_ex, slot, 7)
-    low_join(0, low_got)
-    low_got = low_ring(1, dev_b)
+    exchange(o_own, o_ex, slot, s_sem.at[4], (r_sem.at[7], r_sem.at[8]))
+    wo_t[...] = wo_v[...].astype(F32).T.astype(BF16)
+    low_join(0, 7)
+    low_ring(1, dev_b)
     outs = []
+    take(o_ex, len(NEAR_RING) * SLOT, r_sem.at[7])
     for k in NEAR_RING:
-        got[k].wait_recv()
         outs.append(o_ex[slot(k)].astype(F32))
     res, row = merge([res, new_o] + outs, [row, new_row] + [stat_of(p) for p in outs])
     outs = []
+    take(o_ex, len(FAR_RING) * SLOT, r_sem.at[8])
     for k in FAR_RING:
-        got[k].wait_recv()
         outs.append(o_ex[slot(k)].astype(F32))
     res, row = merge([res] + outs, [row] + [stat_of(p) for p in outs])
     o_all[slot(mine)] = jnp.where(iota((SLOT, HD), 0) < ROWS, res, 0.0).astype(BF16)
-    got = gather(o_all, slot, 15)
-    low_join(1, low_got)
-    low_last = send(low_own.at[2], low_in.at[14], low_s.at[14], low_r.at[14], cross_a(0))
-    for one in got:
-        one.wait_recv()
+    gather(o_all, slot, s_sem.at[5], r_sem.at[9])
+    low_join(1, 7)
+    send(low_own.at[2], low_in.at[14], s_sem.at[7], r_sem.at[13], cross_a(0))
+    take(o_all, 15 * SLOT, r_sem.at[9])
 
     attn = jnp.concatenate([o_all[slot(h)] for h in range(HEADS)], axis=1)
     term = jnp.dot(attn, wo_t[...], preferred_element_type=F32).astype(BF16)
     cols = term.shape[1]
     x_own[:, :cols] = term
-    got = [
-        send(x_own, x_in.at[slot(k - 1)], x_s.at[k - 1], x_r.at[k - 1], dev_x(k))
-        for k in (2, 1, 3)
-    ][::-1]
-    low_join(2, [low_last])
+    for k in (2, 1, 3):
+        send(x_own, x_in.at[slot(k - 1)], s_sem.at[6], r_sem.at[10], dev_x(k))
+    low_join(2, 1)
     for r in range(REQ):
         pair = r // 2
         mass = lse_all[pair] - low_own[3, pair : pair + 1]
@@ -416,15 +402,19 @@
             at_lane = (r % 2) * (HD // 2) + s * HEADS
             moved = pltpu.roll(mass, HD - at_lane, 1) if at_lane else mass
             mass_o[s, :, r, :] = moved[:n_local, :HEADS]
-    for one in got:
-        one.wait_recv()
+    take(x_in, 3 * SLOT, r_sem.at[10])
     term = term.astype(F32)
     for k in range(1, 4):
         term = term + x_in[slot(k - 1), :cols].astype(F32)
     for s in range(STEPS):
         out_o[s] = term[s * REQ : (s + 1) * REQ].astype(BF16)
-    for one in sends:
-        one.wait_send()
+    for i, (ref, rows) in enumerate(
+        (
+            (q_rs, 15 * ROWS), (q_ex, 7 * ROWS), (q_all, 15 * ROWS), (o_rs, 15 * SLOT),
+            (o_ex, 7 * SLOT), (o_all, 15 * SLOT), (x_in, 3 * SLOT), (low_in, 15),
+        )
+    ):
+        take(ref, rows, s_sem.at[i])
 
 
 def hand_on(mass_i, out_i, mass_o, out_o, sem):
@@ -479,7 +469,7 @@
         + [pltpu.VMEM((REQ // 2, SLOT, HD), F32)]
         + [slots(n, BF16) for n in (16, 15, 1, 7, 16, 1, 3)]
         + [pltpu.VMEM((n, REQ // 2, HD), F32) for n in (4, 15)]
-        + [dma(n) for n in (10, 30, 30, 14, 14, 30, 30, 3, 3, 15, 15)],
+        + [dma(n) for n in (10, 8, 14)],
         compiler_params=pltpu.CompilerParams(
             collective_id=0, has_side_effects=True, vmem_limit_bytes=32 * 2**20
         ),

time: 51.1 us -> 49.5 us (0.969)
  Pallas kernels: 50.3 us -> 48.8 us
    pallas_call x1, Pallas kernels: 49.7 us -> 48.1 us  [body(): pl.pallas_call(run, out_shape=shapes, in_specs=[pl.BlockSpec(memory_space...]
where the time goes in v6:
time: 49.5 us; the launch traced here: 49.4 us
  Pallas kernels  48.8 us (99%)
  between operations  0.64 us (1%)
    pallas_call x1, Pallas kernels, body(): pl.pallas_call(run, out_shape=shapes, in_specs=[pl.BlockSpec(memory_space...  48.1 us

profile of v6, /device:TPU:1, one launch (start us, length us, event | category | flops | bytes accessed | tf_op | source)
XLA Modules:
  0.0 49.4 jit_solution(7043122948326093168)
XLA Ops:
  0.6 48.1 %decode.1 = (f32[3,12,4,16]{3,2,1,0:T(4,128)S(1)}, bf16[3,4,32]{2,1,0:T(4,128)(2,1)S(1)}) custom-call(bf16[3,4,32]{2,1,0:T(4,128)(2,1)} %refs_0_.1, bf16[32,2048]{1,0:T(8,128)(2,1)} %refs_1_.1, f32[128]{0:T(128)} %refs_2_.1, f32[1,128,128]{2,1,0:T(8,128)} %refs_3_.1, bf16[4,1,1536,128]{3,2,1,0:T(8,128)(2,1)} %refs_4_.1, bf16[4,1,1536,128]{3,2,1,0:T(8,128)(2,1)} %refs_5_.1, ...), custom_call_target="tpu_custom_call" | custom-call | tf_op jit(solution)/shard_map/decode/pallas_call | solution.py:452
  48.7 0.7 %hand_on.1 = (f32[3,12,4,16]{3,2,1,0:T(4,128)}, bf16[3,4,32]{2,1,0:T(4,128)(2,1)}) custom-call(f32[3,12,4,16]{3,2,1,0:T(4,128)S(1)} %get-tuple-element.6.mass_i, bf16[3,4,32]{2,1,0:T(4,128)(2,1)S(1)} %get-tuple-element.7.out_i), custom_call_target="tpu_custom_call" | custom-call | tf_op jit(solution)/shard_map/hand_on/pallas_call | solution.py:478

commit v7 on v6

--- a/solution.py
+++ b/solution.py
@@ -123,6 +123,13 @@
     def dev_x(k):
         return (ctx, lax.rem(x + k, 4))
 
+    pairs = (
+        (hid_h, hid_v), (wq_h, wq_v), (gain_h, gain_v), (basis_h, basis_v), (lists_h, lists_v),
+        (nk_h, nk_v), (nv_h, nv_v), (wo_h, wo_v), (keys_h, keys_v), (vals_h, vals_v),
+    )
+    fetch = [pltpu.make_async_copy(s, d, in_sem.at[i]) for i, (s, d) in enumerate(pairs)]
+    for one in fetch[:2]:
+        one.start()
     barrier = pltpu.get_barrier_semaphore()
     partners = []
     for k in FAR_FIRST:
@@ -130,12 +137,7 @@
     partners += [dev_x(2), dev_x(1), dev_x(3), cross_a(0)]
     for who in partners:
         pl.semaphore_signal(barrier, inc=1, device_id=who, device_id_type=MESH)
-    pairs = (
-        (hid_h, hid_v), (wq_h, wq_v), (gain_h, gain_v), (basis_h, basis_v), (lists_h, lists_v),
-        (nk_h, nk_v), (nv_h, nv_v), (wo_h, wo_v), (keys_h, keys_v), (vals_h, vals_v),
-    )
-    fetch = [pltpu.make_async_copy(s, d, in_sem.at[i]) for i, (s, d) in enumerate(pairs)]
-    for one in fetch:
+    for one in fetch[2:]:
         one.start()
 
 
@@ -260,12 +262,6 @@
         bias[:, blk * BLK : (blk + 1) * BLK] = jnp.broadcast_to(
             jnp.where(hit > 0.5, 0.0, NONE), (SLOT, BLK)
         )
-    copies = (iota((HD, HD), 0) == lax.rem(iota((HD, HD), 1), RANK)).astype(F32).astype(BF16)
-    for r in range(REQ):
-        low_keys[r // 2, :, (r % 2) * HD : (r % 2 + 1) * HD] = jnp.dot(
-            keys_v[r], copies, preferred_element_type=F32
-        ).astype(BF16)
-
     take(q_all, 15 * ROWS, r_sem.at[4])
 
     lane16 = iota((HEADS, HD), 1)
@@ -278,22 +274,28 @@
         for r in range(REQ)
     ]
     parts_of = [split3(q) for q in q_of]
+    exact_of = []
     for r in range(REQ):
         scores = jnp.dot(
             jnp.concatenate(parts_of[r], axis=0), keys_t[r], preferred_element_type=F32
         )
         scores = scores[:n_rows] + scores[n_rows : 2 * n_rows] + scores[2 * n_rows :]
-        exact = jnp.concatenate(
-            [
-                scores[s * HEADS : (s + 1) * HEADS] + bias[s * REQ + r : s * REQ + r + 1, :]
-                for s in range(STEPS)
-            ],
-            axis=0,
-        )
+        exact_of.append(
+            jnp.concatenate(
+                [
+                    scores[s * HEADS : (s + 1) * HEADS] + bias[s * REQ + r : s * REQ + r + 1, :]
+                    for s in range(STEPS)
+                ],
+                axis=0,
+            )
+        )
+    soft_of = []
+    for exact in exact_of:
         top = jnp.max(exact, axis=1, keepdims=True)
         probs = jnp.exp(exact - top)
-        mass = jnp.sum(probs, axis=1, keepdims=True)
-        acc = jnp.dot(probs.astype(BF16), vals_v[r], preferred_element_type=F32) / mass
+        soft_of.append((top, probs.astype(BF16), jnp.sum(probs, axis=1, keepdims=True)))
+    for r, (top, probs, mass) in enumerate(soft_of):
+        acc = jnp.dot(probs, vals_v[r], preferred_element_type=F32) / mass
         lse = top + jnp.log(mass)
         for s in range(STEPS):
             i = s * REQ + r
@@ -306,6 +308,11 @@
     o_part[...] = o_wide[...].astype(BF16)
 
     scatter(o_part, o_rs, slot, s_sem.at[3], (r_sem.at[5], r_sem.at[6]))
+    copies = (iota((HD, HD), 0) == lax.rem(iota((HD, HD), 1), RANK)).astype(F32).astype(BF16)
+    for r in range(REQ):
+        low_keys[r // 2, :, (r % 2) * HD : (r % 2 + 1) * HD] = jnp.dot(
+            keys_v[r], copies, preferred_element_type=F32
+        ).astype(BF16)
     lane48 = iota((n_rows, HD), 1)
     for pair in range(REQ // 2):
         sides = []
@@ -388,8 +395,13 @@
     send(low_own.at[2], low_in.at[14], s_sem.at[7], r_sem.at[13], cross_a(0))
     take(o_all, 15 * SLOT, r_sem.at[9])
 
-    attn = jnp.concatenate([o_all[slot(h)] for h in range(HEADS)], axis=1)
-    term = jnp.dot(attn, wo_t[...], preferred_element_type=F32).astype(BF16)
+    terms = []
+    for g in range(0, HEADS, 4):
+        attn = jnp.concatenate([o_all[slot(h)] for h in range(g, g + 4)], axis=1)
+        terms.append(
+            jnp.dot(attn, wo_t[g * HD : (g + 4) * HD, :], preferred_element_type=F32)
+        )
+    term = ((terms[0] + terms[1]) + (terms[2] + terms[3])).astype(BF16)
     cols = term.shape[1]
     x_own[:, :cols] = term
     for k in (2, 1, 3):

time: 49.5 us -> 48.7 us (0.984)
  Pallas kernels: 48.8 us -> 48 us
    pallas_call x1, Pallas kernels: 48.1 us -> 47.3 us  [body(): pl.pallas_call(run, out_shape=shapes, in_specs=[pl.BlockSpec(memory_space...]
where the time goes in v7:
time: 48.7 us; the launch traced here: 48.6 us
  Pallas kernels  48 us (99%)
  between operations  0.64 us (1%)
    pallas_call x1, Pallas kernels, body(): pl.pallas_call(run, out_shape=shapes, in_specs=[pl.BlockSpec(memory_space...  47.3 us

profile of v7, /device:TPU:1, one launch (start us, length us, event | category | flops | bytes accessed | tf_op | source)
XLA Modules:
  0.0 48.6 jit_solution(8320241374596494799)
XLA Ops:
  0.6 47.3 %decode.1 = (f32[3,12,4,16]{3,2,1,0:T(4,128)S(1)}, bf16[3,4,32]{2,1,0:T(4,128)(2,1)S(1)}) custom-call(bf16[3,4,32]{2,1,0:T(4,128)(2,1)} %refs_0_.1, bf16[32,2048]{1,0:T(8,128)(2,1)} %refs_1_.1, f32[128]{0:T(128)} %refs_2_.1, f32[1,128,128]{2,1,0:T(8,128)} %refs_3_.1, bf16[4,1,1536,128]{3,2,1,0:T(8,128)(2,1)} %refs_4_.1, bf16[4,1,1536,128]{3,2,1,0:T(8,128)(2,1)} %refs_5_.1, ...), custom_call_target="tpu_custom_call" | custom-call | tf_op jit(solution)/shard_map/decode/pallas_call | solution.py:464
  48.0 0.7 %hand_on.1 = (f32[3,12,4,16]{3,2,1,0:T(4,128)}, bf16[3,4,32]{2,1,0:T(4,128)(2,1)}) custom-call(f32[3,12,4,16]{3,2,1,0:T(4,128)S(1)} %get-tuple-element.6.mass_i, bf16[3,4,32]{2,1,0:T(4,128)(2,1)S(1)} %get-tuple-element.7.out_i), custom_call_target="tpu_custom_call" | custom-call | tf_op jit(solution)/shard_map/hand_on/pallas_call | solution.py:490

commit v8 on v7

--- a/solution.py
+++ b/solution.py
@@ -133,8 +133,9 @@
     barrier = pltpu.get_barrier_semaphore()
     partners = []
     for k in FAR_FIRST:
-        partners += [dev_a(k), dev_b(k), cross_a(k)]
-    partners += [dev_x(2), dev_x(1), dev_x(3), cross_a(0)]
+        partners += [dev_a(k), cross_a(k), dev_b(k)]
+        partners += {5: [dev_x(2)], 6: [dev_x(1), dev_x(3)]}.get(k, [])
+    partners.append(cross_a(0))
     for who in partners:
         pl.semaphore_signal(barrier, inc=1, device_id=who, device_id_type=MESH)
     for one in fetch[2:]:
@@ -305,7 +306,7 @@
     for i, piece in enumerate(split3(stat)):
         o_wide[pl.ds(STAT + i, HEADS, stride=SLOT), :] = piece.astype(F32)
     o_wide[pl.ds(SLOT - 1, HEADS, stride=SLOT), :] = jnp.zeros((HEADS, HD), F32)
-    o_part[...] = o_wide[...].astype(BF16)
+    o_part[...] = o_wide[: HEADS * SLOT].astype(BF16)
 
     scatter(o_part, o_rs, slot, s_sem.at[3], (r_sem.at[5], r_sem.at[6]))
     copies = (iota((HD, HD), 0) == lax.rem(iota((HD, HD), 1), RANK)).astype(F32).astype(BF16)
@@ -477,7 +478,7 @@
             pltpu.VMEM((REQ, HD, n_tok), BF16),
             pltpu.VMEM((REQ // 2, n_tok, 2 * HD), BF16),
         ]
-        + [slots(n) for n in (16, 15, 1, 7, 16, 16)]
+        + [slots(n) for n in (16, 15, 1, 7, 17, 17)]
         + [pltpu.VMEM((REQ // 2, SLOT, HD), F32)]
         + [slots(n, BF16) for n in (16, 15, 1, 7, 16, 1, 3)]
         + [pltpu.VMEM((n, REQ // 2, HD), F32) for n in (4, 15)]

time: 48.7 us -> 48.7 us (level)
  no operation moved by 1% of the time
where the time goes in v8:
time: 48.7 us; the launch traced here: 48.6 us
  Pallas kernels  48 us (99%)
  between operations  0.64 us (1%)
    pallas_call x1, Pallas kernels, body(): pl.pallas_call(run, out_shape=shapes, in_specs=[pl.BlockSpec(memory_space...  47.3 us

profile of v8, /device:TPU:1, one launch (start us, length us, event | category | flops | bytes accessed | tf_op | source)
XLA Modules:
  0.0 48.6 jit_solution(2280824854372770883)
XLA Ops:
  0.6 47.3 %decode.1 = (f32[3,12,4,16]{3,2,1,0:T(4,128)S(1)}, bf16[3,4,32]{2,1,0:T(4,128)(2,1)S(1)}) custom-call(bf16[3,4,32]{2,1,0:T(4,128)(2,1)} %refs_0_.1, bf16[32,2048]{1,0:T(8,128)(2,1)} %refs_1_.1, f32[128]{0:T(128)} %refs_2_.1, f32[1,128,128]{2,1,0:T(8,128)} %refs_3_.1, bf16[4,1,1536,128]{3,2,1,0:T(8,128)(2,1)} %refs_4_.1, bf16[4,1,1536,128]{3,2,1,0:T(8,128)(2,1)} %refs_5_.1, ...), custom_call_target="tpu_custom_call" | custom-call | tf_op jit(solution)/shard_map/decode/pallas_call | solution.py:465
  48.0 0.7 %hand_on.1 = (f32[3,12,4,16]{3,2,1,0:T(4,128)}, bf16[3,4,32]{2,1,0:T(4,128)(2,1)}) custom-call(f32[3,12,4,16]{3,2,1,0:T(4,128)S(1)} %get-tuple-element.6.mass_i, bf16[3,4,32]{2,1,0:T(4,128)(2,1)S(1)} %get-tuple-element.7.out_i), custom_call_target="tpu_custom_call" | custom-call | tf_op jit(solution)/shard_map/hand_on/pallas_call | solution.py:491
